TPU v7x, 128 devices: a whole 4x4x4 slice. The times are simulated.
128 devices in a mesh: box: 16 (over x, z), dir: 8 (over y, core).
Axes of the slice: x: 4, y: 4, z: 4, core: 2. Of those that a mesh axis runs over, the one named last changes fastest.
Arguments:
- coeffs: bfloat16 [2, 64, 32, 8, 128], P(None, 'box', 'dir'), may hold values from -6 to 6
- counts: int32 [64, 32], P('box', 'dir'), may hold values from 0 to 128, as said below
- radiation: bfloat16 [2, 64, 32, 128, 128], P(None, 'box', 'dir'), may hold values from -0.5 to 0.5
- near_blocks: bfloat16 [2, 64, 32, 9, 128, 128], P(None, 'box', 'dir'), may hold values from -0.1875 to 0.1875
- trans_leaf: float32 [2, 7, 7, 128], replicated, may hold values from -0.72 to 0.72
- interp: bfloat16 [512, 128], replicated, may hold values from -0.5 to 0.5
- anterp: bfloat16 [128, 512], replicated, may hold values from -0.25 to 0.25
- shift_angle: float32 [4, 512], replicated, may hold values from -3.140625 to 3.140625
- trans_top: float32 [2, 7, 7, 512], P(None, None, None, ('box', 'dir')), may hold values from -0.6 to 0.6
Outputs:
- field: float32 [2, 64, 32, 8, 128], P(None, 'box', 'dir')
Inputs may be any that keep to these rules, and one draw needn't show every extreme that they name: `counts`: A box with count 0 is empty; some box holds exactly 128 unknowns.
All inputs are finite; a program needn't handle non-finite values.
Results may differ from a plain program's by a relative error of at most 0.0052.
Values may be sent and summed in bfloat16 or wider, within the bound.
No kernel may reach another device: no remote copies, remote signals or barrier semaphores. Data moves between devices by JAX's collectives and lax.ppermute only.
A program may use at most 128 MiB of HBM per device.

v0:
```python
import jax
import jax.numpy as jnp
from jax import lax
from jax.sharding import PartitionSpec as P


def with_halo(cells, sides, width):
    for axis, dim in sides:
        count = lax.axis_size(axis)
        ends = count - 1
        head = lax.slice_in_dim(cells, 0, width, axis=dim)
        tail = lax.slice_in_dim(cells, cells.shape[dim] - width, cells.shape[dim], axis=dim)
        cells = jnp.concatenate(
            [
                lax.ppermute(tail, axis, [(i, (i + 1) % count) for i in range(ends)]),
                cells,
                lax.ppermute(head, axis, [((i + 1) % count, i) for i in range(ends)]),
            ],
            axis=dim,
        )
    return cells


def far_mask(first, second, shift_x, shift_y):
    par_x = (jnp.arange(first, dtype=jnp.int32) % 2)[:, None]
    par_y = (jnp.arange(second, dtype=jnp.int32) % 2)[None, :]
    keep_x = jnp.abs(jnp.floor_divide(par_x + shift_x, 2)) <= 1
    keep_y = jnp.abs(jnp.floor_divide(par_y + shift_y, 2)) <= 1
    return jnp.where(keep_x & keep_y, 1.0, 0.0).astype(jnp.float32)


def translate(padded, table, first, second):
    total_re = jnp.zeros((first, second) + padded.shape[3:], jnp.float32)
    total_im = jnp.zeros((first, second) + padded.shape[3:], jnp.float32)
    for shift_x in range(-3, 4):
        for shift_y in range(-3, 4):
            if max(abs(shift_x), abs(shift_y)) < 2:
                continue
            source = padded[
                :, 3 + shift_x : 3 + shift_x + first, 3 + shift_y : 3 + shift_y + second
            ].astype(jnp.float32)
            weight = far_mask(first, second, shift_x, shift_y)
            weight = weight.reshape(weight.shape + (1,) * (source.ndim - 3))
            coef_re = table[0, shift_x + 3, shift_y + 3]
            coef_im = table[1, shift_x + 3, shift_y + 3]
            total_re = total_re + weight * (coef_re * source[0] - coef_im * source[1])
            total_im = total_im + weight * (coef_re * source[1] + coef_im * source[0])
    return (total_re, total_im)


def complex_form(form, mats, data, conj_sign):
    real_part = jnp.einsum(form, mats[0], data[0], preferred_element_type=jnp.float32)
    cross_part = jnp.einsum(form, mats[1], data[1], preferred_element_type=jnp.float32)
    mixed_one = jnp.einsum(form, mats[0], data[1], preferred_element_type=jnp.float32)
    mixed_two = jnp.einsum(form, mats[1], data[0], preferred_element_type=jnp.float32)
    return (real_part - conj_sign * cross_part, mixed_one + conj_sign * mixed_two)


def shards(
    coeffs, counts, radiation, near_blocks, trans_leaf, interp, anterp, shift_angle, trans_top
):
    n_box = lax.axis_size("box")
    n_dir = lax.axis_size("dir")
    tile_x = coeffs.shape[1]
    tile_y = coeffs.shape[2]
    rhs = coeffs.shape[3]
    slot_count = coeffs.shape[4]
    wide = interp.shape[0]
    share = trans_top.shape[3]
    half_x = tile_x // 2
    half_y = tile_y // 2
    local_top = half_x * half_y
    slots = jnp.arange(slot_count, dtype=jnp.int32)
    live = (slots[None, None, None, :] < counts[:, :, None, None]).astype(jnp.float32)
    masked = (coeffs.astype(jnp.float32) * live).astype(jnp.bfloat16)
    leaf_re, leaf_im = complex_form("ijpk,ijrp->ijrk", radiation, masked, 1.0)
    leaf = jnp.stack([leaf_re, leaf_im]).astype(jnp.bfloat16)
    near_halo = with_halo(masked, (("box", 1), ("dir", 2)), 1)
    far_halo = with_halo(leaf, (("box", 1), ("dir", 2)), 3)
    shifted = jnp.stack(
        [near_halo[:, sx : sx + tile_x, sy : sy + tile_y] for sx in range(3) for sy in range(3)],
        axis=3,
    )
    near_re, near_im = complex_form("ijnqp,ijnrp->ijrq", near_blocks, shifted, 1.0)
    far_re, far_im = translate(far_halo, trans_leaf, tile_x, tile_y)
    spread = jnp.einsum("aijrk,ek->aijre", leaf, interp, preferred_element_type=jnp.float32)
    cosine = jnp.cos(shift_angle).reshape(2, 1, 2, 1, wide)
    sine = jnp.sin(shift_angle).reshape(2, 1, 2, 1, wide)
    grouped = spread.reshape(2, half_x, 2, half_y, 2, rhs, wide)
    up_re = jnp.sum(cosine * grouped[0] - sine * grouped[1], axis=(1, 3))
    up_im = jnp.sum(cosine * grouped[1] + sine * grouped[0], axis=(1, 3))
    upper = jnp.stack([up_re, up_im]).astype(jnp.bfloat16)
    moved = lax.all_to_all(
        upper.reshape(2, 1, local_top, rhs, wide),
        ("box", "dir"),
        split_axis=4,
        concat_axis=1,
        tiled=True,
    )
    grid = moved.reshape(2, n_box, n_dir, half_x, half_y, rhs, share).transpose(0, 1, 3, 2, 4, 5, 6)
    grid = grid.reshape(2, n_box * half_x, n_dir * half_y, rhs * share)
    table = jnp.tile(trans_top, (1, 1, 1, rhs))
    padded_top = jnp.pad(grid, ((0, 0), (3, 3), (3, 3), (0, 0)))
    top_re, top_im = translate(padded_top, table, n_box * half_x, n_dir * half_y)
    top = jnp.stack([top_re, top_im]).astype(jnp.bfloat16)
    outgoing = top.reshape(2, n_box, half_x, n_dir, half_y, rhs, share).transpose(
        0, 1, 3, 2, 4, 5, 6
    )
    returned = lax.all_to_all(
        outgoing.reshape(2, n_box * n_dir, local_top, rhs, share),
        ("box", "dir"),
        split_axis=1,
        concat_axis=4,
        tiled=True,
    )
    parent = returned.reshape(2, half_x, half_y, rhs, wide).astype(jnp.float32)[:, :, None, :, None]
    down_re = (cosine * parent[0] + sine * parent[1]).reshape(tile_x, tile_y, rhs, wide)
    down_im = (cosine * parent[1] - sine * parent[0]).reshape(tile_x, tile_y, rhs, wide)
    down = jnp.stack([down_re, down_im]).astype(jnp.bfloat16)
    back = jnp.einsum("aijre,ke->aijrk", down, anterp, preferred_element_type=jnp.float32)
    total = (jnp.stack([far_re, far_im]) + back).astype(jnp.bfloat16)
    recv_re, recv_im = complex_form("ijpk,ijrk->ijrp", radiation, total, -1.0)
    return jnp.stack([near_re + recv_re, near_im + recv_im]) * live[None]


def solution(mesh):
    return jax.shard_map(
        shards,
        mesh=mesh,
        in_specs=(
            P(None, "box", "dir", None, None),
            P("box", "dir"),
            P(None, "box", "dir", None, None),
            P(None, "box", "dir", None, None, None),
            P(),
            P(),
            P(),
            P(),
            P(None, None, None, ("box", "dir")),
        ),
        out_specs=P(None, "box", "dir", None, None),
        check_vma=False,
    )
```

profile of v0, /device:TPU:1, one launch (start us, length us, event | category | flops | bytes accessed | tf_op | source)
XLA Modules:
  0.0 139.6 jit_solution(16827218454906759690)
XLA Ops:
  0.0 0.8 fusion.115
  0.8 0.9 multiply_convert_fusion
  1.7 4.4 %collective-permute-start = (bf16[2,1,4,8,128]{4,3,2,1,0:T(8,128)(2,1)S(1)}, bf16[2,1,4,8,128]{4,3,2,1,0:T(8,128)(2,1)S(1)}, u32[]{:S(2)}, u32[]{:S(2)}) collective-permute-start(bf16[2,1,4,8,128]{4,3,2,1,0:T(8,128)(2,1)S(1)} %get-tuple-element.105), channel_id=1, source_target_pairs={{0,8},{8,16},{16,24},{24,32},{32,40},{40,48},{48,56},{56,64},{64,7... | collective-permute-start | bytes 49160 | tf_op jit(solution)/shard_map/ppermute | solution.py:15
  6.1 1.3 collective-permute-start.1
  7.4 1.3 fusion.47
  8.6 1.3 fusion.45
  9.9 1.3 fusion.38
  11.3 1.3 fusion.37
  12.6 4.2 %collective-permute-start.4 = (bf16[2,3,4,8,128]{4,3,2,1,0:T(8,128)(2,1)S(1)}, bf16[2,3,4,8,128]{4,3,2,1,0:T(8,128)(2,1)S(1)}, u32[]{:S(2)}, u32[]{:S(2)}) collective-permute-start(bf16[2,3,4,8,128]{4,3,2,1,0:T(8,128)(2,1)S(1)} %get-tuple-element.103), channel_id=1, source_target_pairs={{0,8},{8,16},{16,24},{24,32},{32,40},{40,48},{48,56},{56,64},{64,7... | collective-permute-start | bytes 147464 | tf_op jit(solution)/shard_map/ppermute | solution.py:15
  16.8 1.3 collective-permute-start.5
  18.1 0.8 fusion.122
  19.3 0.7 copy.57
  20.0 1.7 %reshape.3737 = bf16[128,2,128]{2,1,0:T(2,128)(2,1)} reshape(bf16[512,1,2,4,8]{4,3,2,1,0:T(4,128)(2,1)S(1)} %bitcast.508) | data formatting | bytes 131072
  21.7 12.8 %all-to-all-start = ((bf16[128,2,128]{2,1,0:T(2,128)(2,1)}), bf16[128,2,128]{2,1,0:T(2,128)(2,1)S(1)}, u32[]{:S(2)}, u32[]{:S(2)}) async-start(bf16[128,2,128]{2,1,0:T(2,128)(2,1)} %reshape.3737), calls=%async_computation | async-start | bytes 131072 | tf_op jit(solution)/shard_map/all_to_all | solution.py:93
  34.7 0.7 slice_bitcast_fusion.181
  35.3 0.7 slice_bitcast_fusion.182
  39.7 0.7 slice_bitcast_fusion.103
  40.4 0.9 and_select_fusion.97
  41.3 1.1 and_select_fusion.39
  43.0 3.0 %collective-permute-start.3 = (bf16[2,6,1,8,128]{4,3,2,1,0:T(8,128)(2,1)S(1)}, bf16[2,6,1,8,128]{4,3,2,1,0:T(8,128)(2,1)S(1)}, u32[]{:S(2)}, u32[]{:S(2)}) collective-permute-start(bf16[2,6,1,8,128]{4,3,2,1,0:T(8,128)(2,1)S(1)} %get-tuple-element.99), channel_id=1, source_target_pairs={{1,0},{2,1},{3,2},{4,3},{5,4},{6,5},{7,6},{9,8},{10,9},{11,10},{12... | collective-permute-start | bytes 73736 | tf_op jit(solution)/shard_map/ppermute | solution.py:17
  46.0 2.6 %collective-permute-start.2 = (bf16[2,6,1,8,128]{4,3,2,1,0:T(8,128)(2,1)S(1)}, bf16[2,6,1,8,128]{4,3,2,1,0:T(8,128)(2,1)S(1)}, u32[]{:S(2)}, u32[]{:S(2)}) collective-permute-start(bf16[2,6,1,8,128]{4,3,2,1,0:T(8,128)(2,1)S(1)} %get-tuple-element.100), channel_id=1, source_target_pairs={{0,1},{1,2},{2,3},{3,4},{4,5},{5,6},{6,7},{8,9},{9,10},{10,11},{11... | collective-permute-start | bytes 73736 | tf_op jit(solution)/shard_map/ppermute | solution.py:15
  50.8 3.9 %fusion.16 = f32[4,4,8,128]{3,2,1,0:T(8,128)S(1)} fusion(bf16[2,4,4,9,128,128]{5,4,3,2,1,0:T(8,128)(2,1)} %param.12, bf16[2,4,4,9,8,128]{5,4,3,2,1,0:T(8,128)(2,1)S(1)} %fusion.103), kind=kOutput, calls=%fused_computation.56 | convolution fusion | flops 37748736 | bytes 5079040 | tf_op jit(solution)/shard_map/ijnqp,ijnrp->ijrq/dot_general | solution.py:54
  54.7 3.9 %fusion.13 = f32[4,4,8,128]{3,2,1,0:T(8,128)S(1)} fusion(bf16[2,4,4,9,128,128]{5,4,3,2,1,0:T(8,128)(2,1)} %param.12, bf16[2,4,4,9,8,128]{5,4,3,2,1,0:T(8,128)(2,1)S(1)} %fusion.103), kind=kOutput, calls=%fused_computation.55 | convolution fusion | flops 37748736 | bytes 5079040 | tf_op jit(solution)/shard_map/ijnqp,ijnrp->ijrq/dot_general | solution.py:52
  58.7 2.1 %fusion.29 = f32[4,4,8,128]{3,2,1,0:T(8,128)} fusion(f32[4,4,8,128]{3,2,1,0:T(8,128)S(1)} %fusion.16, bf16[2,4,4,9,128,128]{5,4,3,2,1,0:T(8,128)(2,1)S(1)} %copy-done.1, bf16[2,4,4,9,8,128]{5,4,3,2,1,0:T(8,128)(2,1)S(1)} %fusion.103), kind=kOutput, calls=%fused_computation.69 | convolution fusion | flops 37765120 | bytes 5144576 | tf_op jit(solution)/shard_map/ijnqp,ijnrp->ijrq/dot_general | solution.py:55
  60.8 2.1 %fusion.32 = f32[4,4,8,128]{3,2,1,0:T(8,128)} fusion(f32[4,4,8,128]{3,2,1,0:T(8,128)S(1)} %fusion.13, bf16[2,4,4,9,128,128]{5,4,3,2,1,0:T(8,128)(2,1)S(1)} %copy-done.1, bf16[2,4,4,9,8,128]{5,4,3,2,1,0:T(8,128)(2,1)S(1)} %fusion.103), kind=kOutput, calls=%fused_computation.70 | convolution fusion | flops 37765120 | bytes 5144576 | tf_op jit(solution)/shard_map/ijnqp,ijnrp->ijrq/dot_general | solution.py:53
  62.9 0.7 fusion.120
  63.7 3.2 %collective-permute-start.6 = (bf16[2,10,3,8,128]{4,3,2,1,0:T(8,128)(2,1)}, bf16[2,10,3,8,128]{4,3,2,1,0:T(8,128)(2,1)}, u32[]{:S(2)}, u32[]{:S(2)}) collective-permute-start(bf16[2,10,3,8,128]{4,3,2,1,0:T(8,128)(2,1)} %get-tuple-element.91), channel_id=1, source_target_pairs={{0,1},{1,2},{2,3},{3,4},{4,5},{5,6},{6,7},{8,9},{9,10},{10,11},{11... | collective-permute-start | bytes 368648 | tf_op jit(solution)/shard_map/ppermute | solution.py:15
  66.9 1.9 %collective-permute-start.7 = (bf16[2,10,3,8,128]{4,3,2,1,0:T(8,128)(2,1)}, bf16[2,10,3,8,128]{4,3,2,1,0:T(8,128)(2,1)}, u32[]{:S(2)}, u32[]{:S(2)}) collective-permute-start(bf16[2,10,3,8,128]{4,3,2,1,0:T(8,128)(2,1)} %get-tuple-element.92), channel_id=1, source_target_pairs={{1,0},{2,1},{3,2},{4,3},{5,4},{6,5},{7,6},{9,8},{10,9},{11,10},{12... | collective-permute-start | bytes 368648 | tf_op jit(solution)/shard_map/ppermute | solution.py:17
  69.5 1.2 reshape.3738
  70.8 8.1 %copy.76 = bf16[2,16,8,2,2,8,4]{6,5,4,2,3,1,0:T(8,128)(2,1)S(1)} copy(bf16[2,16,8,2,2,8,4]{5,6,2,1,4,3,0:T(4,128)(2,1)S(1)} %bitcast.507) | data formatting | bytes 131072 | tf_op jit(solution)/shard_map/transpose | solution.py:100
  78.9 1.4 %reshape.3728 = bf16[2,32,16,32]{3,2,1,0:T(8,128)(2,1)S(1)} reshape(bf16[2,16,2,8,2,8,4]{6,5,4,3,2,1,0:T(8,128)(2,1)S(1)} %bitcast.506) | data formatting | bytes 131072 | tf_op jit(solution)/shard_map/reshape | solution.py:101
  80.4 1.1 fusion.76
  82.0 0.9 fusion.57
  83.3 6.5 %add_convert_fusion.2 = bf16[1,32,16,32]{3,2,1,0:T(8,128)(2,1)S(1)} fusion(f32[2,32,16,32]{3,2,1,0:T(8,128)S(1)} %get-tuple-element.88, f32[2,32,16,32]{3,2,1,0:T(8,128)S(1)} %get-tuple-element.87, f32[2,32,16,32]{3,2,1,0:T(8,128)S(1)} %get-tuple-element.86, f32[2,32,16,32]{3,2,1,0:T(8,128)S(1)} %get-tuple-element.85, ...), kind=kLoop, calls=%fused_computation.144 | loop fusion | flops 3276800 | bytes 5367808 | tf_op jit(solution)/shard_map/convert.7
  89.7 6.5 %add_convert_fusion.1 = bf16[1,32,16,32]{3,2,1,0:T(8,128)(2,1)S(1)} fusion(f32[2,32,16,32]{3,2,1,0:T(8,128)S(1)} %get-tuple-element.88, f32[2,32,16,32]{3,2,1,0:T(8,128)S(1)} %get-tuple-element.87, f32[2,32,16,32]{3,2,1,0:T(8,128)S(1)} %get-tuple-element.86, f32[2,32,16,32]{3,2,1,0:T(8,128)S(1)} %get-tuple-element.85, ...), kind=kLoop, calls=%fused_computation.143 | loop fusion | flops 3276800 | bytes 5367808 | tf_op jit(solution)/shard_map/convert.6
  96.9 1.8 %copy.62 = bf16[1,16,2,8,2,8,4]{1,5,6,4,3,2,0:T(8,128)(2,1)S(1)} copy(bf16[1,16,2,8,2,8,4]{6,5,4,3,2,1,0:T(8,128)(2,1)S(1)} %stack.96) | data formatting | bytes 65536 | tf_op jit(solution)/shard_map/stack | solution.py:105
  98.6 0.7 stack.95
  99.3 1.8 %copy.61 = bf16[1,16,2,8,2,8,4]{1,5,6,4,3,2,0:T(8,128)(2,1)S(1)} copy(bf16[1,16,2,8,2,8,4]{6,5,4,3,2,1,0:T(8,128)(2,1)S(1)} %stack.95) | data formatting | bytes 65536 | tf_op jit(solution)/shard_map/stack | solution.py:105
  101.2 2.0 %copy.77 = bf16[2,16,8,2,2,8,4]{5,6,4,3,0,2,1:T(4,128)(2,1)S(1)} copy(bf16[2,16,8,2,2,8,4]{1,5,6,4,2,3,0:T(8,128)(2,1)S(1)} %maximum_bitcast_fusion) | data formatting | bytes 131072 | tf_op jit(solution)/shard_map/reshape | solution.py:110
  103.3 1.7 %reshape.3739 = bf16[128,2,128]{2,1,0:T(2,128)(2,1)} reshape(bf16[128,2,4,4,8]{4,3,2,1,0:T(4,128)(2,1)S(1)} %bitcast.510) | data formatting | bytes 131072
  104.9 10.1 %all-to-all-start.1 = ((bf16[128,2,128]{2,1,0:T(2,128)(2,1)}), bf16[128,2,128]{2,1,0:T(2,128)(2,1)S(1)}, u32[]{:S(2)}, u32[]{:S(2)}) async-start(bf16[128,2,128]{2,1,0:T(2,128)(2,1)} %reshape.3739), calls=%async_computation.1 | async-start | bytes 131072 | tf_op jit(solution)/shard_map/all_to_all | solution.py:109
  115.1 9.4 %all-to-all-done.1 = bf16[128,2,128]{2,1,0:T(2,128)(2,1)S(1)} async-done(((bf16[128,2,128]{2,1,0:T(2,128)(2,1)}), bf16[128,2,128]{2,1,0:T(2,128)(2,1)S(1)}, u32[]{:S(2)}, u32[]{:S(2)}) %all-to-all-start.1) | async-done | bytes 65568 | tf_op jit(solution)/shard_map/all_to_all | solution.py:109
  124.5 1.2 reshape.3740
  128.3 1.0 maximum_maximum_fusion
  130.2 3.0 %multiply_add_fusion.1 = f32[1,4,4,8,128]{4,3,2,1,0:T(8,128)S(1)} fusion(f32[2,4,4,8,128]{4,3,2,1,0:T(8,128)S(1)} %get-tuple-element.32, f32[2,4,4,8,128]{4,3,2,1,0:T(8,128)S(1)} %get-tuple-element.33, f32[2,4,4,8,128]{4,3,2,1,0:T(8,128)S(1)} %get-tuple-element.34, f32[2,4,4,8,128]{4,3,2,1,0:T(8,128)S(1)} %get-tuple-element.96, ...), kind=kLoop, calls=%fused_computation.223 | loop fusion | flops 3260416 | bytes 5351936 | tf_op jit(solution)/shard_map/add | solution.py:46
  133.2 2.9 %multiply_add_fusion = f32[1,4,4,8,128]{4,3,2,1,0:T(8,128)S(1)} fusion(f32[2,4,4,8,128]{4,3,2,1,0:T(8,128)S(1)} %get-tuple-element.32, f32[2,4,4,8,128]{4,3,2,1,0:T(8,128)S(1)} %get-tuple-element.33, f32[2,4,4,8,128]{4,3,2,1,0:T(8,128)S(1)} %get-tuple-element.34, f32[2,4,4,8,128]{4,3,2,1,0:T(8,128)S(1)} %get-tuple-element.96, ...), kind=kLoop, calls=%fused_computation.222 | loop fusion | flops 3260416 | bytes 5351936 | tf_op jit(solution)/shard_map/add | solution.py:47
  136.2 1.1 fusion.12
  138.9 0.7 maximum_multiply_fusion
  (260 shorter events, 13.2 us)
Async XLA Ops:
  0.0 18.9 %copy-start = (bf16[512,128]{1,0:T(8,128)(2,1)S(1)}, bf16[512,128]{1,0:T(8,128)(2,1)}, u32[]{:S(2)}) copy-start(bf16[512,128]{1,0:T(8,128)(2,1)} %param.14) | copy-start | bytes 393220
  0.0 34.7 %copy-start.51 = (f32[2,7,7,128]{3,0,2,1:T(2,128)S(1)}, f32[2,7,7,128]{3,0,2,1:T(2,128)}, u32[]{:S(2)}) copy-start(f32[2,7,7,128]{3,0,2,1:T(2,128)} %param.13) | copy-start | bytes 150532
  0.0 37.3 %copy-start.52 = (f32[2,7,7,4]{2,3,1,0:T(4,128)S(1)}, f32[2,7,7,4]{2,3,1,0:T(4,128)}, u32[]{:S(2)}) copy-start(f32[2,7,7,4]{2,3,1,0:T(4,128)} %param.17) | copy-start | bytes 4708
  0.8 49.9 %copy-start.47 = (f32[4,4,128]{2,1,0:T(4,128)}, f32[4,4,128]{2,1,0:T(4,128)S(1)}, u32[]{:S(2)}) copy-start(f32[4,4,128]{2,1,0:T(4,128)S(1)} %fusion.115) | copy-start | bytes 24580
  1.7 41.3 %collective-permute-start = (bf16[2,1,4,8,128]{4,3,2,1,0:T(8,128)(2,1)S(1)}, bf16[2,1,4,8,128]{4,3,2,1,0:T(8,128)(2,1)S(1)}, u32[]{:S(2)}, u32[]{:S(2)}) collective-permute-start(bf16[2,1,4,8,128]{4,3,2,1,0:T(8,128)(2,1)S(1)} %get-tuple-element.105), channel_id=1, source_target_pairs={{0,8},{8,16},{16,24},{24,32},{32,40},{40,48},{48,56},{56,64},{64,7... | collective-permute-start | bytes 49160 | tf_op jit(solution)/shard_map/ppermute | solution.py:15
  6.1 37.0 %collective-permute-start.1 = (bf16[2,1,4,8,128]{4,3,2,1,0:T(8,128)(2,1)S(1)}, bf16[2,1,4,8,128]{4,3,2,1,0:T(8,128)(2,1)S(1)}, u32[]{:S(2)}, u32[]{:S(2)}) collective-permute-start(bf16[2,1,4,8,128]{4,3,2,1,0:T(8,128)(2,1)S(1)} %get-tuple-element.106), channel_id=1, source_target_pairs={{8,0},{16,8},{24,16},{32,24},{40,32},{48,40},{56,48},{64,56},{72,6... | collective-permute-start | bytes 49160 | tf_op jit(solution)/shard_map/ppermute | solution.py:17
  9.9 40.7 %copy-start.6 = (bf16[2,4,4,8,128]{4,3,2,1,0:T(8,128)(2,1)S(1)}, bf16[2,4,4,8,128]{4,3,2,1,0:T(8,128)(2,1)}, u32[]{:S(2)}) copy-start(bf16[2,4,4,8,128]{4,3,2,1,0:T(8,128)(2,1)} %param.9) | copy-start | bytes 196612
  12.6 50.3 %collective-permute-start.4 = (bf16[2,3,4,8,128]{4,3,2,1,0:T(8,128)(2,1)S(1)}, bf16[2,3,4,8,128]{4,3,2,1,0:T(8,128)(2,1)S(1)}, u32[]{:S(2)}, u32[]{:S(2)}) collective-permute-start(bf16[2,3,4,8,128]{4,3,2,1,0:T(8,128)(2,1)S(1)} %get-tuple-element.103), channel_id=1, source_target_pairs={{0,8},{8,16},{16,24},{24,32},{32,40},{40,48},{48,56},{56,64},{64,7... | collective-permute-start | bytes 147464 | tf_op jit(solution)/shard_map/ppermute | solution.py:15
  16.8 46.1 %collective-permute-start.5 = (bf16[2,3,4,8,128]{4,3,2,1,0:T(8,128)(2,1)S(1)}, bf16[2,3,4,8,128]{4,3,2,1,0:T(8,128)(2,1)S(1)}, u32[]{:S(2)}, u32[]{:S(2)}) collective-permute-start(bf16[2,3,4,8,128]{4,3,2,1,0:T(8,128)(2,1)S(1)} %get-tuple-element.104), channel_id=1, source_target_pairs={{8,0},{16,8},{24,16},{32,24},{40,32},{48,40},{56,48},{64,56},{72,6... | collective-permute-start | bytes 147464 | tf_op jit(solution)/shard_map/ppermute | solution.py:17
  21.7 47.8 %all-to-all-start = ((bf16[128,2,128]{2,1,0:T(2,128)(2,1)}), bf16[128,2,128]{2,1,0:T(2,128)(2,1)S(1)}, u32[]{:S(2)}, u32[]{:S(2)}) async-start(bf16[128,2,128]{2,1,0:T(2,128)(2,1)} %reshape.3737), calls=%async_computation | async-start | bytes 131072 | tf_op jit(solution)/shard_map/all_to_all | solution.py:93
  43.0 7.5 %collective-permute-start.3 = (bf16[2,6,1,8,128]{4,3,2,1,0:T(8,128)(2,1)S(1)}, bf16[2,6,1,8,128]{4,3,2,1,0:T(8,128)(2,1)S(1)}, u32[]{:S(2)}, u32[]{:S(2)}) collective-permute-start(bf16[2,6,1,8,128]{4,3,2,1,0:T(8,128)(2,1)S(1)} %get-tuple-element.99), channel_id=1, source_target_pairs={{1,0},{2,1},{3,2},{4,3},{5,4},{6,5},{7,6},{9,8},{10,9},{11,10},{12... | collective-permute-start | bytes 73736 | tf_op jit(solution)/shard_map/ppermute | solution.py:17
  46.0 4.5 %collective-permute-start.2 = (bf16[2,6,1,8,128]{4,3,2,1,0:T(8,128)(2,1)S(1)}, bf16[2,6,1,8,128]{4,3,2,1,0:T(8,128)(2,1)S(1)}, u32[]{:S(2)}, u32[]{:S(2)}) collective-permute-start(bf16[2,6,1,8,128]{4,3,2,1,0:T(8,128)(2,1)S(1)} %get-tuple-element.100), channel_id=1, source_target_pairs={{0,1},{1,2},{2,3},{3,4},{4,5},{5,6},{6,7},{8,9},{9,10},{10,11},{11... | collective-permute-start | bytes 73736 | tf_op jit(solution)/shard_map/ppermute | solution.py:15
  50.8 7.9 %copy-start.1 = (bf16[2,4,4,9,128,128]{5,4,3,2,1,0:T(8,128)(2,1)S(1)}, bf16[2,4,4,9,128,128]{5,4,3,2,1,0:T(8,128)(2,1)}, u32[]{:S(2)}) copy-start(bf16[2,4,4,9,128,128]{5,4,3,2,1,0:T(8,128)(2,1)} %param.12) | copy-start | bytes 28311556
  63.7 64.6 %collective-permute-start.6 = (bf16[2,10,3,8,128]{4,3,2,1,0:T(8,128)(2,1)}, bf16[2,10,3,8,128]{4,3,2,1,0:T(8,128)(2,1)}, u32[]{:S(2)}, u32[]{:S(2)}) collective-permute-start(bf16[2,10,3,8,128]{4,3,2,1,0:T(8,128)(2,1)} %get-tuple-element.91), channel_id=1, source_target_pairs={{0,1},{1,2},{2,3},{3,4},{4,5},{5,6},{6,7},{8,9},{9,10},{10,11},{11... | collective-permute-start | bytes 368648 | tf_op jit(solution)/shard_map/ppermute | solution.py:15
  66.9 61.3 %collective-permute-start.7 = (bf16[2,10,3,8,128]{4,3,2,1,0:T(8,128)(2,1)}, bf16[2,10,3,8,128]{4,3,2,1,0:T(8,128)(2,1)}, u32[]{:S(2)}, u32[]{:S(2)}) collective-permute-start(bf16[2,10,3,8,128]{4,3,2,1,0:T(8,128)(2,1)} %get-tuple-element.92), channel_id=1, source_target_pairs={{1,0},{2,1},{3,2},{4,3},{5,4},{6,5},{7,6},{9,8},{10,9},{11,10},{12... | collective-permute-start | bytes 368648 | tf_op jit(solution)/shard_map/ppermute | solution.py:17
  96.2 18.8 %copy-start.3 = (bf16[2,7,4,8,128]{4,3,2,1,0:T(8,128)(2,1)S(1)}, bf16[2,7,4,8,128]{4,3,2,1,0:T(8,128)(2,1)}, u32[]{:S(2)}) copy-start(bf16[2,7,4,8,128]{4,3,2,1,0:T(8,128)(2,1)} %get-tuple-element.102) | copy-start | bytes 344068
  104.9 19.6 %all-to-all-start.1 = ((bf16[128,2,128]{2,1,0:T(2,128)(2,1)}), bf16[128,2,128]{2,1,0:T(2,128)(2,1)S(1)}, u32[]{:S(2)}, u32[]{:S(2)}) async-start(bf16[128,2,128]{2,1,0:T(2,128)(2,1)} %reshape.3739), calls=%async_computation.1 | async-start | bytes 131072 | tf_op jit(solution)/shard_map/all_to_all | solution.py:109
  127.7 2.1 %copy-start.53 = (f32[4,4]{1,0:T(4,128)S(1)}, f32[4,4]{1,0:T(4,128)}, u32[]{:S(2)}) copy-start(f32[4,4]{1,0:T(4,128)} %get-tuple-element.271) | copy-start | bytes 196
  127.7 2.1 %copy-start.54 = (f32[4,4]{1,0:T(4,128)S(1)}, f32[4,4]{1,0:T(4,128)}, u32[]{:S(2)}) copy-start(f32[4,4]{1,0:T(4,128)} %get-tuple-element.272) | copy-start | bytes 196
  127.7 2.1 %copy-start.55 = (f32[4,4]{1,0:T(4,128)S(1)}, f32[4,4]{1,0:T(4,128)}, u32[]{:S(2)}) copy-start(f32[4,4]{1,0:T(4,128)} %get-tuple-element.305) | copy-start | bytes 196
  127.7 2.1 %copy-start.56 = (f32[4,4]{1,0:T(4,128)S(1)}, f32[4,4]{1,0:T(4,128)}, u32[]{:S(2)}) copy-start(f32[4,4]{1,0:T(4,128)} %get-tuple-element.306) | copy-start | bytes 196
  127.8 2.1 %copy-start.57 = (f32[4,4]{1,0:T(4,128)S(1)}, f32[4,4]{1,0:T(4,128)}, u32[]{:S(2)}) copy-start(f32[4,4]{1,0:T(4,128)} %get-tuple-element.307) | copy-start | bytes 196
  127.8 2.1 %copy-start.58 = (f32[4,4]{1,0:T(4,128)S(1)}, f32[4,4]{1,0:T(4,128)}, u32[]{:S(2)}) copy-start(f32[4,4]{1,0:T(4,128)} %get-tuple-element.308) | copy-start | bytes 196
  127.8 2.1 %copy-start.59 = (f32[4,4]{1,0:T(4,128)S(1)}, f32[4,4]{1,0:T(4,128)}, u32[]{:S(2)}) copy-start(f32[4,4]{1,0:T(4,128)} %get-tuple-element.309) | copy-start | bytes 196
  127.8 2.1 %copy-start.60 = (f32[4,4]{1,0:T(4,128)S(1)}, f32[4,4]{1,0:T(4,128)}, u32[]{:S(2)}) copy-start(f32[4,4]{1,0:T(4,128)} %get-tuple-element.310) | copy-start | bytes 196
  127.8 2.1 %copy-start.61 = (f32[4,4]{1,0:T(4,128)S(1)}, f32[4,4]{1,0:T(4,128)}, u32[]{:S(2)}) copy-start(f32[4,4]{1,0:T(4,128)} %get-tuple-element.311) | copy-start | bytes 196
  127.8 2.1 %copy-start.62 = (f32[4,4]{1,0:T(4,128)S(1)}, f32[4,4]{1,0:T(4,128)}, u32[]{:S(2)}) copy-start(f32[4,4]{1,0:T(4,128)} %get-tuple-element.312) | copy-start | bytes 196
  127.8 2.1 %copy-start.63 = (f32[4,4]{1,0:T(4,128)S(1)}, f32[4,4]{1,0:T(4,128)}, u32[]{:S(2)}) copy-start(f32[4,4]{1,0:T(4,128)} %get-tuple-element.313) | copy-start | bytes 196
  127.8 2.1 %copy-start.64 = (f32[4,4]{1,0:T(4,128)S(1)}, f32[4,4]{1,0:T(4,128)}, u32[]{:S(2)}) copy-start(f32[4,4]{1,0:T(4,128)} %get-tuple-element.314) | copy-start | bytes 196
  127.8 2.1 %copy-start.65 = (f32[4,4]{1,0:T(4,128)S(1)}, f32[4,4]{1,0:T(4,128)}, u32[]{:S(2)}) copy-start(f32[4,4]{1,0:T(4,128)} %get-tuple-element.315) | copy-start | bytes 196
  127.8 2.1 %copy-start.66 = (f32[4,4]{1,0:T(4,128)S(1)}, f32[4,4]{1,0:T(4,128)}, u32[]{:S(2)}) copy-start(f32[4,4]{1,0:T(4,128)} %get-tuple-element.316) | copy-start | bytes 196
  127.8 2.1 %copy-start.67 = (f32[4,4]{1,0:T(4,128)S(1)}, f32[4,4]{1,0:T(4,128)}, u32[]{:S(2)}) copy-start(f32[4,4]{1,0:T(4,128)} %get-tuple-element.317) | copy-start | bytes 196
  127.9 2.1 %copy-start.68 = (f32[4,4]{1,0:T(4,128)S(1)}, f32[4,4]{1,0:T(4,128)}, u32[]{:S(2)}) copy-start(f32[4,4]{1,0:T(4,128)} %get-tuple-element.318) | copy-start | bytes 196
  127.9 2.1 %copy-start.69 = (f32[4,4]{1,0:T(4,128)S(1)}, f32[4,4]{1,0:T(4,128)}, u32[]{:S(2)}) copy-start(f32[4,4]{1,0:T(4,128)} %get-tuple-element.319) | copy-start | bytes 196
  127.9 2.1 %copy-start.70 = (f32[4,4]{1,0:T(4,128)S(1)}, f32[4,4]{1,0:T(4,128)}, u32[]{:S(2)}) copy-start(f32[4,4]{1,0:T(4,128)} %get-tuple-element.320) | copy-start | bytes 196
  127.9 2.1 %copy-start.71 = (f32[4,4]{1,0:T(4,128)S(1)}, f32[4,4]{1,0:T(4,128)}, u32[]{:S(2)}) copy-start(f32[4,4]{1,0:T(4,128)} %get-tuple-element.321) | copy-start | bytes 196
  127.9 2.1 %copy-start.72 = (f32[4,4]{1,0:T(4,128)S(1)}, f32[4,4]{1,0:T(4,128)}, u32[]{:S(2)}) copy-start(f32[4,4]{1,0:T(4,128)} %get-tuple-element.322) | copy-start | bytes 196
  127.9 2.1 %copy-start.73 = (f32[4,4]{1,0:T(4,128)S(1)}, f32[4,4]{1,0:T(4,128)}, u32[]{:S(2)}) copy-start(f32[4,4]{1,0:T(4,128)} %get-tuple-element.323) | copy-start | bytes 196
  127.9 2.1 %copy-start.74 = (f32[4,4]{1,0:T(4,128)S(1)}, f32[4,4]{1,0:T(4,128)}, u32[]{:S(2)}) copy-start(f32[4,4]{1,0:T(4,128)} %get-tuple-element.324) | copy-start | bytes 196
  127.9 2.1 %copy-start.75 = (f32[4,4]{1,0:T(4,128)S(1)}, f32[4,4]{1,0:T(4,128)}, u32[]{:S(2)}) copy-start(f32[4,4]{1,0:T(4,128)} %get-tuple-element.325) | copy-start | bytes 196
  127.9 2.1 %copy-start.76 = (f32[4,4]{1,0:T(4,128)S(1)}, f32[4,4]{1,0:T(4,128)}, u32[]{:S(2)}) copy-start(f32[4,4]{1,0:T(4,128)} %get-tuple-element.326) | copy-start | bytes 196
  128.0 2.1 %copy-start.77 = (f32[4,4]{1,0:T(4,128)S(1)}, f32[4,4]{1,0:T(4,128)}, u32[]{:S(2)}) copy-start(f32[4,4]{1,0:T(4,128)} %get-tuple-element.327) | copy-start | bytes 196
  128.0 2.1 %copy-start.78 = (f32[4,4]{1,0:T(4,128)S(1)}, f32[4,4]{1,0:T(4,128)}, u32[]{:S(2)}) copy-start(f32[4,4]{1,0:T(4,128)} %get-tuple-element.328) | copy-start | bytes 196
  128.0 2.1 %copy-start.79 = (f32[4,4]{1,0:T(4,128)S(1)}, f32[4,4]{1,0:T(4,128)}, u32[]{:S(2)}) copy-start(f32[4,4]{1,0:T(4,128)} %get-tuple-element.329) | copy-start | bytes 196
  130.2 7.1 %copy-start.2 = (bf16[2,4,4,128,128]{4,3,2,1,0:T(8,128)(2,1)S(1)}, bf16[2,4,4,128,128]{4,3,2,1,0:T(8,128)(2,1)}, u32[]{:S(2)}) copy-start(bf16[2,4,4,128,128]{4,3,2,1,0:T(8,128)(2,1)} %param.11) | copy-start | bytes 3145732
  133.2 4.9 %copy-start.5 = (f32[4,4,8,128]{3,2,1,0:T(8,128)S(1)}, f32[4,4,8,128]{3,2,1,0:T(8,128)}, u32[]{:S(2)}) copy-start(f32[4,4,8,128]{3,2,1,0:T(8,128)} %fusion.29) | copy-start | bytes 196612
  133.2 5.3 %copy-start.4 = (f32[4,4,8,128]{3,2,1,0:T(8,128)S(1)}, f32[4,4,8,128]{3,2,1,0:T(8,128)}, u32[]{:S(2)}) copy-start(f32[4,4,8,128]{3,2,1,0:T(8,128)} %fusion.32) | copy-start | bytes 196612
  133.2 5.7 %copy-start.48 = (f32[4,4,128]{2,1,0:T(4,128)S(1)}, f32[4,4,128]{2,1,0:T(4,128)}, u32[]{:S(2)}) copy-start(f32[4,4,128]{2,1,0:T(4,128)} %copy-done.47) | copy-start | bytes 24580
  (54 other events, 81.6 us)
where the time goes:
time: 140 us
  starting transfers between devices  44.7 us (32%)
  local copies, waits for them, and re-layouts  34.6 us (25%)
  other arithmetic  28.7 us (20%)
  matrix products  20.2 us (14%)
  waiting for transfers between devices  9.43 us (7%)
  between operations  1.94 us (1%)
    ppermute x4, starting transfers between devices, with_halo(): lax.ppermute(tail, axis, [(i, (i + 1) % count) for i in range(ends)])  14.4 us
    another operation x3, other arithmetic  13 us
    all_to_all x1, starting transfers between devices, shards(): lax.all_to_all(upper.reshape(2, 1, local_top, rhs, wide), ('box', 'dir'),...  12.8 us
    all_to_all x1, starting transfers between devices, shards(): lax.all_to_all(outgoing.reshape(2, n_box * n_dir, local_top, rhs, share),...  10.1 us
    all_to_all x1, waiting for transfers between devices, shards(): lax.all_to_all(outgoing.reshape(2, n_box * n_dir, local_top, rhs, share),...  9.41 us
    transpose x1, local copies, waits for them, and re-layouts, shards(): moved.reshape(2, n_box, n_dir, half_x, half_y, rhs, share)  8.07 us
    ppermute x4, starting transfers between devices, with_halo(): lax.ppermute(head, axis, [((i + 1) % count, i) for i in range(ends)])  7.48 us
    mul x10, local copies, waits for them, and re-layouts, translate(): total_re = total_re + weight * (coef_re * source[0] - coef_im * source[1])  6.5 us
  transfers between devices with their start and end apart: 10, of which 1 were waited for; matrix products, arithmetic and copies ran while one was open for 51% of the time, Pallas kernels for 0%

commit v1 on v0

v1 whole, which is shorter than its diff:
```python
import jax
import jax.numpy as jnp
from jax import lax
from jax.experimental import pallas as pl
from jax.experimental.pallas import tpu as pltpu
from jax.sharding import PartitionSpec as P

OWN, EDGE, SIDE = 48, 28, 70
NT = (((1,), (1,)), ((), ()))
F32 = jnp.float32
BF16 = jnp.bfloat16
LINK = F32
LEAF_VMEM = 62 << 20


def dot_nt(left, right):
    return lax.dot_general(left, right, NT, preferred_element_type=F32)


def pair(real, imag):
    return jnp.concatenate([real, imag], axis=0)


def vmem():
    return pl.BlockSpec(memory_space=pltpu.VMEM)


def smem():
    return pl.BlockSpec(memory_space=pltpu.SMEM)


def hbm():
    return pl.BlockSpec(memory_space=pl.ANY)


def params(mib):
    return pltpu.CompilerParams(vmem_limit_bytes=mib << 20)


def cost(us):
    return pl.CostEstimate(flops=us * 10**9, bytes_accessed=us << 20, transcendentals=0)


def leaf_kernel(
    counts_hbm,
    coeffs_hbm,
    radiation,
    interp_hbm,
    angle_hbm,
    table_hbm,
    own,
    up,
    down,
    phase,
    piece,
    counts,
    coeffs,
    rad,
    interp,
    angle,
    table,
    sems,
    rad_sems,
):
    small = [
        pltpu.make_async_copy(counts_hbm, counts, sems.at[0]),
        pltpu.make_async_copy(coeffs_hbm, coeffs, sems.at[1]),
        pltpu.make_async_copy(angle_hbm, angle, sems.at[2]),
        pltpu.make_async_copy(interp_hbm, interp, sems.at[3]),
        pltpu.make_async_copy(table_hbm, table, sems.at[4]),
    ]
    copies = [
        pltpu.make_async_copy(radiation.at[:, i], rad.at[:, i], rad_sems.at[i]) for i in range(4)
    ]
    for copy in small + copies:
        copy.start()
    for copy in small:
        copy.wait()
    cosine = jnp.cos(angle[...])
    sine = jnp.sin(angle[...])
    phase[0:4, :] = cosine
    phase[4:8, :] = sine
    piece[...] = jnp.zeros_like(piece)
    for part in range(2):
        for dx in range(7):
            at = (part * 7 + dx) * 8
            piece[:, at : at + 7] = table[part, dx].astype(piece.dtype)
    lane = lax.broadcasted_iota(jnp.int32, (16, 128), 1)
    leaves = []
    for copy in copies:
        copy.wait()
    for i in range(4):
        for j in range(4):
            both = pair(coeffs[0, i, j].astype(F32), coeffs[1, i, j].astype(F32))
            masked = jnp.where(lane < counts[i, j], both, 0.0).astype(BF16)
            wide = jnp.concatenate([rad[0, i, j], rad[1, i, j]], axis=1)
            prod = jnp.dot(masked, wide, preferred_element_type=F32)
            first, second = prod[:, 0:128], prod[:, 128:256]
            leaf = pair(first[0:8] - second[8:16], first[8:16] + second[0:8]).astype(BF16)
            leaves.append(leaf)
            own[j * 4 + i] = leaf
            own[16 + j * 4 + i] = masked
            if i < 2:
                down[j * 2 + i] = leaf
            else:
                up[j * 2 + i - 2] = leaf
            if i == 0:
                down[8 + j] = masked
            if i == 3:
                up[8 + j] = masked
    spread = dot_nt(jnp.concatenate(leaves, axis=0), interp[...])
    for big_i in range(2):
        for big_j in range(2):
            real = imag = None
            for a in range(2):
                for b in range(2):
                    at = ((2 * big_i + a) * 4 + 2 * big_j + b) * 16
                    s_re, s_im = spread[at : at + 8], spread[at + 8 : at + 16]
                    c = cosine[2 * a + b : 2 * a + b + 1]
                    s = sine[2 * a + b : 2 * a + b + 1]
                    t_re = c * s_re - s * s_im
                    t_im = c * s_im + s * s_re
                    real = t_re if real is None else real + t_re
                    imag = t_im if imag is None else imag + t_im
            upper = pair(real, imag).astype(BF16)
            for t in range(4):
                unit = (big_i * 2 + big_j) * 4 + t
                tile = upper[:, t * 128 : (t + 1) * 128]
                own[32 + unit] = tile
                up[12 + unit] = tile
                down[12 + unit] = tile


def pieces_kernel(piece, pieces):
    pieces[...] = jnp.broadcast_to(piece[...][None], pieces.shape)


def pack_kernel(own, before, after, right, left, sem):
    copies = []
    for target, col in ((right, 2), (left, 0)):
        edge_col = 3 if col else 0
        moves = [
            (before.at[pl.ds(col * 2, 4)], 0, 4),
            (own.at[pl.ds(col * 4, 8)], 4, 8),
            (after.at[pl.ds(col * 2, 4)], 12, 4),
            (before.at[pl.ds(8 + edge_col, 1)], 16, 1),
            (own.at[pl.ds(16 + edge_col * 4, 4)], 17, 4),
            (after.at[pl.ds(8 + edge_col, 1)], 21, 1),
            (before.at[pl.ds(12, 16)], 22, 16),
            (own.at[pl.ds(32, 16)], 38, 16),
            (after.at[pl.ds(12, 16)], 54, 16),
        ]
        for source, at, size in moves:
            copies.append((source, target.at[pl.ds(at, size)]))
    started = [
        pltpu.make_async_copy(source, target, sem.at[index])
        for index, (source, target) in enumerate(copies)
    ]
    for copy in started:
        copy.start()
    for copy in started:
        copy.wait()


def near_sum(masks, real_blocks, imag_blocks):
    row = jnp.concatenate(masks, axis=1)
    first = dot_nt(row, jnp.concatenate(real_blocks, axis=1))
    second = dot_nt(row, jnp.concatenate(imag_blocks, axis=1))
    return pair(first[0:8] - second[8:16], first[8:16] + second[0:8])


def inside(j):
    return [dy for dy in (-1, 0, 1) if 0 <= j + dy < 4]


def near_kernel(own, before, after, blocks, out, held, sems):
    copies = []
    for i in range(4):
        group = [pltpu.make_async_copy(blocks.at[:, i, 1:3], held.at[:, i, 1:3], sems.at[i, 0])]
        for j, low in ((0, 1), (3, 0)):
            for dx in range(3):
                span = pl.ds(3 * dx + low, 2)
                group.append(
                    pltpu.make_async_copy(
                        blocks.at[:, i, j, span], held.at[:, i, j, span], sems.at[i, len(group)]
                    )
                )
        copies.append(group)
    for group in copies:
        for copy in group:
            copy.start()
    here = lax.axis_index("box")
    has_before = (here > 0).astype(F32)
    has_after = (here < lax.axis_size("box") - 1).astype(F32)
    rows = {}
    for j in range(4):
        rows[-1, j] = (before[8 + j].astype(F32) * has_before).astype(BF16)
        rows[4, j] = (after[8 + j].astype(F32) * has_after).astype(BF16)
        for i in range(4):
            rows[i, j] = own[16 + j * 4 + i]
    for i in range(4):
        for copy in copies[i]:
            copy.wait()
        for j in range(4):
            pairs = [(dx, dy) for dx in (-1, 0, 1) for dy in inside(j)]
            out[i * 4 + j] = near_sum(
                [rows[i + dx, j + dy] for dx, dy in pairs],
                [held[0, i, j, 3 * (dx + 1) + dy + 1] for dx, dy in pairs],
                [held[1, i, j, 3 * (dx + 1) + dy + 1] for dx, dy in pairs],
            )


def translate(source, coef, keep):
    total = {}
    for r in range(6):
        for c in range(6):
            unit = source(r, c)
            s_re, s_im = unit[0:8], unit[8:16]
            for a in range(2):
                for b in range(2):
                    dx, dy = r - 2 - a, c - 2 - b
                    if max(abs(dx), abs(dy)) < 2:
                        continue
                    k_re, k_im = coef(0, dx, dy), coef(1, dx, dy)
                    t_re = k_re * s_re - k_im * s_im
                    t_im = k_re * s_im + k_im * s_re
                    if (a, b) in total:
                        old_re, old_im = total[a, b]
                        t_re, t_im = old_re + t_re, old_im + t_im
                    total[a, b] = (t_re, t_im)
    for (a, b), (t_re, t_im) in total.items():
        keep(a, b, pair(t_re, t_im))


def final_kernel(
    counts,
    own,
    before,
    after,
    left,
    right,
    pieces,
    trans_leaf,
    anterp,
    phase,
    near,
    rad,
    blocks,
    out,
    rest,
    leaf_halo,
    upper_halo,
    table,
    far,
    top,
    sems,
):
    copies = []
    for i in range(4):
        for dx in range(3):
            for side, (j, n) in enumerate(((0, 3 * dx), (3, 3 * dx + 2))):
                slot = (i * 3 + dx) * 2 + side
                copies.append(
                    pltpu.make_async_copy(blocks.at[:, i, j, n], rest.at[:, slot], sems.at[slot])
                )
    for copy in copies:
        copy.start()
    box, col = lax.axis_index("box"), lax.axis_index("dir")
    f_before = (box > 0).astype(F32)
    f_after = (box < lax.axis_size("box") - 1).astype(F32)
    f_left = (col > 0).astype(F32)
    f_right = (col < lax.axis_size("dir") - 1).astype(F32)

    for j in range(4):
        for r in range(2):
            leaf_halo[r * 8 + j + 2] = before[j * 2 + r].astype(F32) * f_before
            leaf_halo[(r + 6) * 8 + j + 2] = after[j * 2 + r].astype(F32) * f_after
        for i in range(4):
            leaf_halo[(i + 2) * 8 + j + 2] = own[j * 4 + i].astype(F32)
    for part, flag, start in ((left, f_left, 0), (right, f_right, 6)):
        for c in range(2):
            for r in range(2):
                leaf_halo[r * 8 + start + c] = part[c * 2 + r].astype(F32) * (flag * f_before)
                leaf_halo[(r + 6) * 8 + start + c] = part[12 + c * 2 + r].astype(F32) * (
                    flag * f_after
                )
            for i in range(4):
                leaf_halo[(i + 2) * 8 + start + c] = part[4 + c * 4 + i].astype(F32) * flag
    for p in range(2):
        for q in range(2):
            for t in range(4):
                unit = (p * 2 + q) * 4 + t
                upper_halo[t, p * 6 + q + 2] = before[12 + unit].astype(F32) * f_before
                upper_halo[t, (p + 2) * 6 + q + 2] = own[32 + unit].astype(F32)
                upper_halo[t, (p + 4) * 6 + q + 2] = after[12 + unit].astype(F32) * f_after
                for part, flag, start in ((left, f_left, 0), (right, f_right, 4)):
                    upper_halo[t, p * 6 + q + start] = part[22 + unit].astype(F32) * (
                        flag * f_before
                    )
                    upper_halo[t, (p + 2) * 6 + q + start] = part[38 + unit].astype(F32) * flag
                    upper_halo[t, (p + 4) * 6 + q + start] = part[54 + unit].astype(F32) * (
                        flag * f_after
                    )
    for t in range(4):
        table[t] = pieces[pl.ds(t * 32, 32)].astype(F32).reshape(128, 128).T

    def leaf_step(quad, carry):
        base = (quad // 2) * 16 + (quad % 2) * 2

        def keep(a, b, value):
            far[quad * 4 + a * 2 + b] = value

        translate(
            lambda r, c: leaf_halo[base + r * 8 + c],
            lambda part, dx, dy: trans_leaf[dx + 3, dy + 3, pl.ds(part, 1), :],
            keep,
        )
        return carry

    def top_step(t, carry):
        def keep(a, b, value):
            top[t, a * 2 + b] = value.astype(BF16).astype(F32)

        translate(
            lambda r, c: upper_halo[t, r * 6 + c],
            lambda part, dx, dy: table[t, pl.ds((part * 7 + dx + 3) * 8 + dy + 3, 1), :],
            keep,
        )
        return carry

    lax.fori_loop(0, 4, leaf_step, 0)
    lax.fori_loop(0, 4, top_step, 0)

    rows = []
    for quad in range(4):
        for child in range(4):
            tiles = []
            for t in range(4):
                unit = top[t, quad]
                t_re, t_im = unit[0:8], unit[8:16]
                c = phase[child : child + 1, t * 128 : (t + 1) * 128]
                s = phase[4 + child : 5 + child, t * 128 : (t + 1) * 128]
                tiles.append(pair(c * t_re + s * t_im, c * t_im - s * t_re).astype(BF16))
            rows.append(jnp.concatenate(tiles, axis=1))
    back = dot_nt(jnp.concatenate(rows, axis=0), anterp[...])
    lane = lax.broadcasted_iota(jnp.int32, (16, 128), 1)
    for copy in copies:
        copy.wait()

    def side_mask(part, flag, i):
        if i < 0:
            return (part[16].astype(F32) * (flag * f_before)).astype(BF16)
        if i > 3:
            return (part[21].astype(F32) * (flag * f_after)).astype(BF16)
        return (part[17 + i].astype(F32) * flag).astype(BF16)

    sides = {}
    for i in range(-1, 5):
        sides[0, i] = side_mask(left, f_left, i)
        sides[3, i] = side_mask(right, f_right, i)
    for i in range(4):
        for j in range(4):
            at = ((i // 2) * 2 + j // 2) * 4 + (i % 2) * 2 + j % 2
            total = (far[at] + back[at * 16 : at * 16 + 16]).astype(BF16)
            both = dot_nt(total, rad[:, i, j].reshape(256, 128))
            first, second = both[:, 0:128], both[:, 128:256]
            field = near[i * 4 + j] + pair(
                first[0:8] + second[8:16], first[8:16] - second[0:8]
            )
            if j in (0, 3):
                slots = [(i * 3 + dx) * 2 + (1 if j else 0) for dx in range(3)]
                field = field + near_sum(
                    [sides[j, i + dx] for dx in (-1, 0, 1)],
                    [rest[0, slot] for slot in slots],
                    [rest[1, slot] for slot in slots],
                )
            field = jnp.where(lane < counts[i, j], field, 0.0)
            out[0, i, j] = field[0:8]
            out[1, i, j] = field[8:16]


def unit_shape(count):
    return jax.ShapeDtypeStruct((count, 16, 128), BF16)


def shards(
    coeffs, counts, radiation, near_blocks, trans_leaf, interp, anterp, shift_angle, trans_top
):
    n_box = lax.axis_size("box")
    n_dir = lax.axis_size("dir")
    devices = n_box * n_dir
    own, to_after, to_before, phase, piece = pl.pallas_call(
        leaf_kernel,
        out_shape=(
            unit_shape(OWN),
            unit_shape(EDGE),
            unit_shape(EDGE),
            jax.ShapeDtypeStruct((8, 512), F32),
            jax.ShapeDtypeStruct((4, 128), LINK),
        ),
        in_specs=[hbm()] * 6,
        out_specs=(vmem(),) * 5,
        scratch_shapes=[
            pltpu.SMEM((4, 4), jnp.int32),
            pltpu.VMEM((2, 4, 4, 8, 128), BF16),
            pltpu.VMEM((2, 4, 4, 128, 128), BF16),
            pltpu.VMEM((512, 128), BF16),
            pltpu.VMEM((4, 512), F32),
            pltpu.VMEM((2, 7, 4, 7), F32),
            pltpu.SemaphoreType.DMA((5,)),
            pltpu.SemaphoreType.DMA((4,)),
        ],
        compiler_params=pltpu.CompilerParams(vmem_limit_bytes=LEAF_VMEM),
        cost_estimate=cost(2),
        name="leaf",
    )(counts, coeffs, radiation, interp, shift_angle, trans_top.transpose(0, 1, 3, 2))
    forward = [(i, (i + 1) % n_box) for i in range(n_box)]
    backward = [((i + 1) % n_box, i) for i in range(n_box)]
    before = lax.ppermute(to_after, "box", forward)
    after = lax.ppermute(to_before, "box", backward)
    pieces = pl.pallas_call(
        pieces_kernel,
        out_shape=jax.ShapeDtypeStruct((devices, 4, 128), LINK),
        in_specs=[vmem()],
        out_specs=vmem(),
        compiler_params=params(4),
        cost_estimate=cost(20),
        name="pieces",
    )(piece)
    gathered = lax.all_to_all(pieces, ("box", "dir"), split_axis=0, concat_axis=0, tiled=True)
    to_right, to_left = pl.pallas_call(
        pack_kernel,
        out_shape=(unit_shape(SIDE), unit_shape(SIDE)),
        in_specs=[hbm()] * 3,
        out_specs=(hbm(),) * 2,
        scratch_shapes=[pltpu.SemaphoreType.DMA((18,))],
        compiler_params=params(4),
        cost_estimate=cost(20),
        name="pack",
    )(own, before, after)
    left = lax.ppermute(to_right, "dir", [(i, (i + 1) % n_dir) for i in range(n_dir)])
    right = lax.ppermute(to_left, "dir", [((i + 1) % n_dir, i) for i in range(n_dir)])
    near = pl.pallas_call(
        near_kernel,
        out_shape=jax.ShapeDtypeStruct((16, 16, 128), F32),
        in_specs=[vmem()] * 3 + [hbm()],
        out_specs=vmem(),
        scratch_shapes=[
            pltpu.VMEM((2, 4, 4, 9, 128, 128), BF16),
            pltpu.SemaphoreType.DMA((4, 7)),
        ],
        compiler_params=params(48),
        cost_estimate=cost(4),
        name="near",
    )(own, before, after, near_blocks)
    return pl.pallas_call(
        final_kernel,
        out_shape=jax.ShapeDtypeStruct((2, 4, 4, 8, 128), F32),
        in_specs=[smem()] + [vmem()] * 11 + [hbm()],
        out_specs=vmem(),
        scratch_shapes=[
            pltpu.VMEM((2, 24, 128, 128), BF16),
            pltpu.VMEM((64, 16, 128), F32),
            pltpu.VMEM((4, 36, 16, 128), F32),
            pltpu.VMEM((4, 128, 128), F32),
            pltpu.VMEM((16, 16, 128), F32),
            pltpu.VMEM((4, 4, 16, 128), F32),
            pltpu.SemaphoreType.DMA((24,)),
        ],
        compiler_params=params(48),
        cost_estimate=cost(4),
        name="final",
    )(
        counts,
        own,
        before,
        after,
        left,
        right,
        gathered,
        trans_leaf.transpose(1, 2, 0, 3),
        anterp,
        phase,
        near,
        radiation,
        near_blocks,
    )


def solution(mesh):
    return jax.shard_map(
        shards,
        mesh=mesh,
        in_specs=(
            P(None, "box", "dir", None, None),
            P("box", "dir"),
            P(None, "box", "dir", None, None),
            P(None, "box", "dir", None, None, None),
            P(),
            P(),
            P(),
            P(),
            P(None, None, None, ("box", "dir")),
        ),
        out_specs=P(None, "box", "dir", None, None),
        check_vma=False,
    )
```

time: 140 us -> 32.5 us (0.23)
  local copies, waits for them, and re-layouts: 34.6 us -> 0.7 us
  starting transfers between devices: 44.7 us -> 15.2 us
  other arithmetic: 28.7 us -> 0 us
  matrix products: 20.2 us -> 0 us
  Pallas kernels: 0 us -> 12.5 us
  waiting for transfers between devices: 9.43 us -> 3.72 us
  between operations: 1.94 us -> 0.14 us
    dot_general x14 -> x0, matrix products: 20.2 us -> none  [the longest x3 5.61 us: complex_form(): jnp.einsum(form, mats[0], data[1], preferred_element_type=jnp.float32)]
    all_to_all x2 -> x1, starting transfers between devices: 22.9 us -> 6.66 us  [shards(): lax.all_to_all(pieces, ('box', 'dir'), split_axis=0, concat_axis=0, tiled...]
    ppermute x8 -> x4, starting transfers between devices: 21.9 us -> 8.58 us  [the longest x1 4.4 us: shards(): after = lax.ppermute(to_before, 'box', backward)]
    another operation x5 -> x0, other arithmetic: 13 us -> none
    pallas_call x0 -> x5, Pallas kernels: none -> 12.5 us  [the longest x1 4.37 us: shards(): pl.pallas_call(near_kernel, out_shape=jax.ShapeDtypeStruct((16, 16, 128),...]
    mul x20 -> x0, local copies, waits for them, and re-layouts: 8.46 us -> none  [the longest x10 6.5 us: translate(): total_re = total_re + weight * (coef_re * source[0] - coef_im * source[1])]
    transpose x1 -> x0, local copies, waits for them, and re-layouts: 8.07 us -> none  [shards(): moved.reshape(2, n_box, n_dir, half_x, half_y, rhs, share)]
    add x2 -> x0, other arithmetic: 5.9 us -> none  [the longest x1 2.95 us: translate(): total_re = total_re + weight * (coef_re * source[0] - coef_im * source[1])]
  transfers between devices with their start and end apart: 10 -> 5, of which waited for: 1 -> 1; matrix products, arithmetic and copies ran while one was open for 51% -> 0% of each run, Pallas kernels for 0% -> 19%
where the time goes in v1:
time: 32.5 us; the launch traced here: 32.3 us
  starting transfers between devices  15.2 us (47%)
  Pallas kernels  12.5 us (38%)
  waiting for transfers between devices  3.72 us (11%)
  local copies, waits for them, and re-layouts  0.7 us (2%)
    all_to_all x1, starting transfers between devices, shards(): lax.all_to_all(pieces, ('box', 'dir'), split_axis=0, concat_axis=0, tiled...  6.66 us
    ppermute x1, starting transfers between devices, shards(): after = lax.ppermute(to_before, 'box', backward)  4.4 us
    pallas_call x1, Pallas kernels, shards(): pl.pallas_call(near_kernel, out_shape=jax.ShapeDtypeStruct((16, 16, 128),...  4.37 us
    pallas_call x1, Pallas kernels, shards(): pl.pallas_call(final_kernel, out_shape=jax.ShapeDtypeStruct((2, 4, 4, 8,...  3.93 us
    all_to_all x1, waiting for transfers between devices, shards(): lax.all_to_all(pieces, ('box', 'dir'), split_axis=0, concat_axis=0, tiled...  3.71 us
    ppermute x1, starting transfers between devices, shards(): before = lax.ppermute(to_after, 'box', forward)  2.54 us
    pallas_call x1, Pallas kernels, shards(): pl.pallas_call(leaf_kernel, out_shape=(unit_shape(OWN), unit_shape(EDGE),...  2.5 us
    ppermute x1, starting transfers between devices, shards(): lax.ppermute(to_right, 'dir', [(i, (i + 1) % n_dir) for i in range(n_dir)])  1.65 us
  transfers between devices with their start and end apart: 5, of which 1 were waited for; matrix products, arithmetic and copies ran while one was open for 0% of the time, Pallas kernels for 19%

profile of v1, /device:TPU:1, one launch (start us, length us, event | category | flops | bytes accessed | tf_op | source)
XLA Modules:
  0.0 32.3 jit_solution(754250111335845729)
XLA Ops:
  0.0 2.5 %leaf.1 = (bf16[48,16,128]{2,1,0:T(8,128)(2,1)}, bf16[28,16,128]{2,1,0:T(8,128)(2,1)}, bf16[28,16,128]{2,1,0:T(8,128)(2,1)}, f32[8,512]{1,0:T(8,128)}, f32[4,128]{1,0:T(4,128)}) custom-call(s32[4,4]{1,0:T(4,128)} %counts.1, bf16[2,4,4,8,128]{4,3,2,1,0:T(8,128)(2,1)} %coeffs_hbm.1, bf16[2,4,4,128,128]{4,3,2,1,0:T(8,128)(2,1)} %rad.1, ...), custom_call_target="tpu_custom_call" | custom-call | flops 2000000000 | bytes 2097152 | tf_op jit(solution)/shard_map/leaf/pallas_call | solution.py:392
  2.5 2.5 %collective-permute-start = (bf16[28,16,128]{2,1,0:T(8,128)(2,1)}, bf16[28,16,128]{2,1,0:T(8,128)(2,1)S(1)}, u32[]{:S(2)}, u32[]{:S(2)}) collective-permute-start(bf16[28,16,128]{2,1,0:T(8,128)(2,1)} %get-tuple-element.13), channel_id=1, source_target_pairs={{0,8},{8,16},{16,24},{24,32},{32,40},{40,48},{48,56},{56,64},{64,7... | collective-permute-start | bytes 344072 | tf_op jit(solution)/shard_map/ppermute | solution.py:419
  5.0 4.4 %collective-permute-start.1 = (bf16[28,16,128]{2,1,0:T(8,128)(2,1)}, bf16[28,16,128]{2,1,0:T(8,128)(2,1)S(1)}, u32[]{:S(2)}, u32[]{:S(2)}) collective-permute-start(bf16[28,16,128]{2,1,0:T(8,128)(2,1)} %get-tuple-element.14), channel_id=1, source_target_pairs={{8,0},{16,8},{24,16},{32,24},{40,32},{48,40},{56,48},{64,56},{72,6... | collective-permute-start | bytes 344072 | tf_op jit(solution)/shard_map/ppermute | solution.py:420
  9.4 0.0 copy-start.6
  9.4 0.7 %copy-done.6 = f32[4,128]{1,0:T(4,128)S(1)} copy-done((f32[4,128]{1,0:T(4,128)S(1)}, f32[4,128]{1,0:T(4,128)}, u32[]{:S(2)}) %copy-start.6) | copy-done | bytes 2072
  10.1 0.0 copy-start.4
  10.1 0.7 %pieces.1 = f32[128,4,128]{2,1,0:T(4,128)} custom-call(f32[4,128]{1,0:T(4,128)S(1)} %copy-done.6), custom_call_target="tpu_custom_call" | custom-call | flops 20000000000 | bytes 20971520 | tf_op jit(solution)/shard_map/pieces/pallas_call | solution.py:421
  10.9 6.7 %all-to-all-start = ((f32[128,4,128]{2,1,0:T(4,128)}), f32[128,4,128]{2,1,0:T(4,128)S(1)}, u32[]{:S(2)}, u32[]{:S(2)}) async-start(f32[128,4,128]{2,1,0:T(4,128)} %pieces.1), calls=%async_computation | async-start | bytes 524288 | tf_op jit(solution)/shard_map/all_to_all | solution.py:430
  17.5 0.0 collective-permute-done.before
  17.5 0.0 collective-permute-done.1.after
  17.5 0.0 copy-done.4
  17.5 0.9 %pack.1 = (bf16[70,16,128]{2,1,0:T(8,128)(2,1)S(1)}, bf16[70,16,128]{2,1,0:T(8,128)(2,1)S(1)}) custom-call(bf16[48,16,128]{2,1,0:T(8,128)(2,1)S(1)} %copy-done.4, bf16[28,16,128]{2,1,0:T(8,128)(2,1)S(1)} %collective-permute-done.before, bf16[28,16,128]{2,1,0:T(8,128)(2,1)S(1)} %collective-permute-done.1.after), custom_call_target="tpu_custom_call" | custom-call | flops 20000000000 | bytes 20971520 | tf_op jit(solution)/shard_map/pack/pallas_call | solution.py:431
  18.5 0.0 copy-start
  18.5 0.0 copy-start.1
  18.5 0.0 copy-start.2
  18.5 0.0 copy-start.3
  18.5 0.0 copy-start.5
  18.6 1.6 %collective-permute-start.2 = (bf16[70,16,128]{2,1,0:T(8,128)(2,1)S(1)}, bf16[70,16,128]{2,1,0:T(8,128)(2,1)S(1)}, u32[]{:S(2)}, u32[]{:S(2)}) collective-permute-start(bf16[70,16,128]{2,1,0:T(8,128)(2,1)S(1)} %get-tuple-element.15), channel_id=1, source_target_pairs={{0,1},{1,2},{2,3},{3,4},{4,5},{5,6},{6,7},{7,0},{8,9},{9,10},{10,1... | collective-permute-start | bytes 860168 | tf_op jit(solution)/shard_map/ppermute | solution.py:441
  20.2 0.0 collective-permute-start.3
  20.2 4.4 %near.1 = f32[16,16,128]{2,1,0:T(8,128)S(1)} custom-call(bf16[48,16,128]{2,1,0:T(8,128)(2,1)S(1)} %copy-done.4, bf16[28,16,128]{2,1,0:T(8,128)(2,1)S(1)} %collective-permute-done.before, bf16[28,16,128]{2,1,0:T(8,128)(2,1)S(1)} %collective-permute-done.1.after, bf16[2,4,4,9,128,128]{5,4,3,2,1,0:T(8,128)(2,1)} %blocks.3), custom_call_target="tpu_custom_call" | custom-call | flops 4000000000 | bytes 4194304 | tf_op jit(solution)/shard_map/near/pallas_call | solution.py:443
  24.6 3.7 %all-to-all-done.pieces = f32[128,4,128]{2,1,0:T(4,128)S(1)} async-done(((f32[128,4,128]{2,1,0:T(4,128)}), f32[128,4,128]{2,1,0:T(4,128)S(1)}, u32[]{:S(2)}, u32[]{:S(2)}) %all-to-all-start) | async-done | bytes 262176 | tf_op jit(solution)/shard_map/all_to_all | solution.py:430
  28.3 0.0 collective-permute-done.2.left
  28.3 0.0 collective-permute-done.3.right
  28.3 0.0 copy-done
  28.3 0.0 copy-done.1
  28.3 0.0 copy-done.2
  28.3 0.0 copy-done.3
  28.3 0.0 copy-done.5
  28.3 3.9 %final.1 = f32[2,4,4,8,128]{4,3,2,1,0:T(8,128)} custom-call(s32[4,4]{1,0:T(4,128)S(1)} %copy-done.3, bf16[48,16,128]{2,1,0:T(8,128)(2,1)S(1)} %copy-done.4, bf16[28,16,128]{2,1,0:T(8,128)(2,1)S(1)} %collective-permute-done.before, bf16[28,16,128]{2,1,0:T(8,128)(2,1)S(1)} %collective-permute-done.1.after, ...), custom_call_target="tpu_custom_call" | custom-call | flops 4000000000 | bytes 4194304 | tf_op jit(solution)/shard_map/final/pallas_call | solution.py:456
Async XLA Ops:
  2.5 15.0 %collective-permute-start = (bf16[28,16,128]{2,1,0:T(8,128)(2,1)}, bf16[28,16,128]{2,1,0:T(8,128)(2,1)S(1)}, u32[]{:S(2)}, u32[]{:S(2)}) collective-permute-start(bf16[28,16,128]{2,1,0:T(8,128)(2,1)} %get-tuple-element.13), channel_id=1, source_target_pairs={{0,8},{8,16},{16,24},{24,32},{32,40},{40,48},{48,56},{56,64},{64,7... | collective-permute-start | bytes 344072 | tf_op jit(solution)/shard_map/ppermute | solution.py:419
  5.0 12.5 %collective-permute-start.1 = (bf16[28,16,128]{2,1,0:T(8,128)(2,1)}, bf16[28,16,128]{2,1,0:T(8,128)(2,1)S(1)}, u32[]{:S(2)}, u32[]{:S(2)}) collective-permute-start(bf16[28,16,128]{2,1,0:T(8,128)(2,1)} %get-tuple-element.14), channel_id=1, source_target_pairs={{8,0},{16,8},{24,16},{32,24},{40,32},{48,40},{56,48},{64,56},{72,6... | collective-permute-start | bytes 344072 | tf_op jit(solution)/shard_map/ppermute | solution.py:420
  9.4 0.7 %copy-start.6 = (f32[4,128]{1,0:T(4,128)S(1)}, f32[4,128]{1,0:T(4,128)}, u32[]{:S(2)}) copy-start(f32[4,128]{1,0:T(4,128)} %get-tuple-element.17.piece) | copy-start | bytes 6148
  10.1 7.4 %copy-start.4 = (bf16[48,16,128]{2,1,0:T(8,128)(2,1)S(1)}, bf16[48,16,128]{2,1,0:T(8,128)(2,1)}, u32[]{:S(2)}) copy-start(bf16[48,16,128]{2,1,0:T(8,128)(2,1)} %get-tuple-element.12.own) | copy-start | bytes 589828
  10.9 17.4 %all-to-all-start = ((f32[128,4,128]{2,1,0:T(4,128)}), f32[128,4,128]{2,1,0:T(4,128)S(1)}, u32[]{:S(2)}, u32[]{:S(2)}) async-start(f32[128,4,128]{2,1,0:T(4,128)} %pieces.1), calls=%async_computation | async-start | bytes 524288 | tf_op jit(solution)/shard_map/all_to_all | solution.py:430
  18.5 9.8 %copy-start = (bf16[2,4,4,128,128]{4,3,2,1,0:T(8,128)(2,1)S(1)}, bf16[2,4,4,128,128]{4,3,2,1,0:T(8,128)(2,1)}, u32[]{:S(2)}) copy-start(bf16[2,4,4,128,128]{4,3,2,1,0:T(8,128)(2,1)} %rad.1) | copy-start | bytes 3145732
  18.5 9.8 %copy-start.1 = (bf16[128,512]{1,0:T(8,128)(2,1)S(1)}, bf16[128,512]{1,0:T(8,128)(2,1)}, u32[]{:S(2)}) copy-start(bf16[128,512]{1,0:T(8,128)(2,1)} %anterp.1) | copy-start | bytes 393220
  18.5 9.8 %copy-start.2 = (f32[2,7,7,128]{3,0,2,1:T(2,128)S(1)}, f32[2,7,7,128]{3,0,2,1:T(2,128)}, u32[]{:S(2)}) copy-start(f32[2,7,7,128]{3,0,2,1:T(2,128)} %param.13) | copy-start | bytes 150532
  18.5 9.8 %copy-start.3 = (s32[4,4]{1,0:T(4,128)S(1)}, s32[4,4]{1,0:T(4,128)}, u32[]{:S(2)}) copy-start(s32[4,4]{1,0:T(4,128)} %counts.1) | copy-start | bytes 196
  18.5 9.8 %copy-start.5 = (f32[8,512]{1,0:T(8,128)S(1)}, f32[8,512]{1,0:T(8,128)}, u32[]{:S(2)}) copy-start(f32[8,512]{1,0:T(8,128)} %get-tuple-element.18.phase) | copy-start | bytes 49156
  18.6 9.7 %collective-permute-start.2 = (bf16[70,16,128]{2,1,0:T(8,128)(2,1)S(1)}, bf16[70,16,128]{2,1,0:T(8,128)(2,1)S(1)}, u32[]{:S(2)}, u32[]{:S(2)}) collective-permute-start(bf16[70,16,128]{2,1,0:T(8,128)(2,1)S(1)} %get-tuple-element.15), channel_id=1, source_target_pairs={{0,1},{1,2},{2,3},{3,4},{4,5},{5,6},{6,7},{7,0},{8,9},{9,10},{10,1... | collective-permute-start | bytes 860168 | tf_op jit(solution)/shard_map/ppermute | solution.py:441
  20.2 8.1 %collective-permute-start.3 = (bf16[70,16,128]{2,1,0:T(8,128)(2,1)S(1)}, bf16[70,16,128]{2,1,0:T(8,128)(2,1)S(1)}, u32[]{:S(2)}, u32[]{:S(2)}) collective-permute-start(bf16[70,16,128]{2,1,0:T(8,128)(2,1)S(1)} %get-tuple-element.16), channel_id=1, source_target_pairs={{1,0},{2,1},{3,2},{4,3},{5,4},{6,5},{7,6},{0,7},{9,8},{10,9},{11,1... | collective-permute-start | bytes 860168 | tf_op jit(solution)/shard_map/ppermute | solution.py:442

commit v2 on v1

v2 whole, which is shorter than its diff:
```python
import jax
import jax.numpy as jnp
from jax import lax
from jax.experimental import pallas as pl
from jax.experimental.pallas import tpu as pltpu
from jax.sharding import PartitionSpec as P

OWN, EDGE, SIDE = 48, 28, 70
NT = (((1,), (1,)), ((), ()))
F32 = jnp.float32
BF16 = jnp.bfloat16


def dot_nt(left, right):
    return lax.dot_general(left, right, NT, preferred_element_type=F32)


def pair(real, imag):
    return jnp.concatenate([real, imag], axis=0)


def vmem():
    return pl.BlockSpec(memory_space=pltpu.VMEM)


def hbm():
    return pl.BlockSpec(memory_space=pl.ANY)


def params(mib):
    return pltpu.CompilerParams(vmem_limit_bytes=mib << 20)


def cost(us):
    return pl.CostEstimate(flops=us * 10**9, bytes_accessed=us << 20, transcendentals=0)


def leaf_kernel(
    counts_hbm,
    coeffs_hbm,
    radiation,
    interp_hbm,
    angle_hbm,
    table_hbm,
    own_hbm,
    up_hbm,
    down_hbm,
    phase_hbm,
    live_hbm,
    pieces_hbm,
    counts,
    coeffs,
    rad,
    interp,
    angle,
    table,
    own,
    up,
    down,
    phase,
    live,
    pieces,
    sems,
    rad_sems,
    out_sems,
):
    counts_in = pltpu.make_async_copy(counts_hbm, counts, sems.at[0])
    coeffs_in = pltpu.make_async_copy(coeffs_hbm, coeffs, sems.at[1])
    angle_in = pltpu.make_async_copy(angle_hbm, angle, sems.at[2])
    table_in = pltpu.make_async_copy(table_hbm, table, sems.at[3])
    interp_in = pltpu.make_async_copy(interp_hbm, interp, sems.at[4])
    rad_in = [
        pltpu.make_async_copy(radiation.at[:, i], rad.at[:, i], rad_sems.at[i]) for i in range(4)
    ]
    for copy in (table_in, angle_in, counts_in, coeffs_in, *rad_in, interp_in):
        copy.start()
    sent = []

    def send(source, target):
        copy = pltpu.make_async_copy(source, target, out_sems.at[len(sent)])
        copy.start()
        sent.append(copy)

    pieces[0] = jnp.zeros((4, 128), F32)
    table_in.wait()
    for part in range(2):
        for dx in range(7):
            at = (part * 7 + dx) * 8
            pieces[0, :, at : at + 7] = table[part, dx]
    pieces[...] = jnp.broadcast_to(pieces[0:1], pieces.shape)
    send(pieces, pieces_hbm)
    angle_in.wait()
    cosine = jnp.cos(angle[...])
    sine = jnp.sin(angle[...])
    phase[0:4, :] = cosine
    phase[4:8, :] = sine
    send(phase, phase_hbm)
    counts_in.wait()
    lane = lax.broadcasted_iota(jnp.int32, (8, 128), 1)
    for i in range(4):
        for j in range(4):
            live[i * 4 + j] = (lane < counts[i, j]).astype(F32)
    send(live, live_hbm)
    coeffs_in.wait()
    for copy in rad_in:
        copy.wait()
    leaves = []
    for i in range(4):
        for j in range(4):
            on = live[i * 4 + j]
            masked = pair(
                coeffs[0, i, j].astype(F32) * on, coeffs[1, i, j].astype(F32) * on
            ).astype(BF16)
            wide = jnp.concatenate([rad[0, i, j], rad[1, i, j]], axis=1)
            prod = jnp.dot(masked, wide, preferred_element_type=F32)
            first, second = prod[:, 0:128], prod[:, 128:256]
            leaf = pair(first[0:8] - second[8:16], first[8:16] + second[0:8]).astype(BF16)
            leaves.append(leaf)
            own[j * 4 + i] = leaf
            own[16 + j * 4 + i] = masked
            if i < 2:
                down[j * 2 + i] = leaf
            else:
                up[j * 2 + i - 2] = leaf
            if i == 0:
                down[8 + j] = masked
            if i == 3:
                up[8 + j] = masked
    for source, target, count in ((up, up_hbm, 12), (down, down_hbm, 12), (own, own_hbm, 32)):
        send(source.at[pl.ds(0, count)], target.at[pl.ds(0, count)])
    interp_in.wait()
    spread = dot_nt(jnp.concatenate(leaves, axis=0), interp[...])
    for big_i in range(2):
        for big_j in range(2):
            real = imag = None
            for a in range(2):
                for b in range(2):
                    at = ((2 * big_i + a) * 4 + 2 * big_j + b) * 16
                    s_re, s_im = spread[at : at + 8], spread[at + 8 : at + 16]
                    c = cosine[2 * a + b : 2 * a + b + 1]
                    s = sine[2 * a + b : 2 * a + b + 1]
                    t_re = c * s_re - s * s_im
                    t_im = c * s_im + s * s_re
                    real = t_re if real is None else real + t_re
                    imag = t_im if imag is None else imag + t_im
            upper = pair(real, imag).astype(BF16)
            for t in range(4):
                own[32 + (big_i * 2 + big_j) * 4 + t] = upper[:, t * 128 : (t + 1) * 128]
    uppers = own.at[pl.ds(32, 16)]
    for target, at in ((up_hbm, 12), (down_hbm, 12), (own_hbm, 32)):
        send(uppers, target.at[pl.ds(at, 16)])
    for copy in sent:
        copy.wait()


def pass_kernel(pieces, same):
    del pieces, same


def pack_kernel(own, before, after, right, left):
    for target, col in ((right, 2), (left, 0)):
        edge_col = 3 if col else 0
        moves = [
            (before, col * 2, 0, 4),
            (own, col * 4, 4, 8),
            (after, col * 2, 12, 4),
            (before, 8 + edge_col, 16, 1),
            (own, 16 + edge_col * 4, 17, 4),
            (after, 8 + edge_col, 21, 1),
            (before, 12, 22, 16),
            (own, 32, 38, 16),
            (after, 12, 54, 16),
        ]
        for source, start, at, size in moves:
            target[at : at + size] = source[start : start + size]


def near_sum(masks, real_blocks, imag_blocks):
    row = jnp.concatenate(masks, axis=1)
    first = dot_nt(row, jnp.concatenate(real_blocks, axis=1))
    second = dot_nt(row, jnp.concatenate(imag_blocks, axis=1))
    return pair(first[0:8] - second[8:16], first[8:16] + second[0:8])


def masked_unit(unit, flag):
    return (unit.astype(F32) * flag).astype(BF16)


def inside(j):
    return [dy for dy in (-1, 0, 1) if 0 <= j + dy < 4]


def near_kernel(own, before, after, blocks, out, rest, held, sems, rest_sems):
    copies = []
    for i in range(4):
        group = [pltpu.make_async_copy(blocks.at[:, i, 1:3], held.at[:, i, 1:3], sems.at[i, 0])]
        for j, low in ((0, 1), (3, 0)):
            for dx in range(3):
                span = pl.ds(3 * dx + low, 2)
                group.append(
                    pltpu.make_async_copy(
                        blocks.at[:, i, j, span], held.at[:, i, j, span], sems.at[i, len(group)]
                    )
                )
        copies.append(group)
    for group in copies:
        for copy in group:
            copy.start()
    rest_copies = []
    for side, j in enumerate((0, 3)):
        for dx in range(3):
            slot = side * 3 + dx
            rest_copies.append(
                pltpu.make_async_copy(
                    blocks.at[:, :, j, 3 * dx + 2 * side], rest.at[slot], rest_sems.at[slot]
                )
            )
    for copy in rest_copies:
        copy.start()
    here = lax.axis_index("box")
    has_before = (here > 0).astype(F32)
    has_after = (here < lax.axis_size("box") - 1).astype(F32)
    rows = {}
    for j in range(4):
        rows[-1, j] = (before[8 + j].astype(F32) * has_before).astype(BF16)
        rows[4, j] = (after[8 + j].astype(F32) * has_after).astype(BF16)
        for i in range(4):
            rows[i, j] = own[16 + j * 4 + i]
    for i in range(4):
        for copy in copies[i]:
            copy.wait()
        for j in range(4):
            pairs = [(dx, dy) for dx in (-1, 0, 1) for dy in inside(j)]
            out[i * 4 + j] = near_sum(
                [rows[i + dx, j + dy] for dx, dy in pairs],
                [held[0, i, j, 3 * (dx + 1) + dy + 1] for dx, dy in pairs],
                [held[1, i, j, 3 * (dx + 1) + dy + 1] for dx, dy in pairs],
            )
    for copy in rest_copies:
        copy.wait()


def translate(source, coef, keep):
    total = {}
    for r in range(6):
        for c in range(6):
            unit = source(r, c)
            s_re, s_im = unit[0:8], unit[8:16]
            for a in range(2):
                for b in range(2):
                    dx, dy = r - 2 - a, c - 2 - b
                    if max(abs(dx), abs(dy)) < 2:
                        continue
                    k_re, k_im = coef(0, dx, dy), coef(1, dx, dy)
                    t_re = k_re * s_re - k_im * s_im
                    t_im = k_re * s_im + k_im * s_re
                    if (a, b) in total:
                        old_re, old_im = total[a, b]
                        t_re, t_im = old_re + t_re, old_im + t_im
                    total[a, b] = (t_re, t_im)
    for (a, b), (t_re, t_im) in total.items():
        keep(a, b, pair(t_re, t_im))


def middle_kernel(
    own,
    before,
    after,
    left,
    right,
    trans_leaf,
    near,
    rest,
    far,
    upper_halo,
    field,
    leaf_halo,
):
    box, col = lax.axis_index("box"), lax.axis_index("dir")
    f_before = (box > 0).astype(F32)
    f_after = (box < lax.axis_size("box") - 1).astype(F32)
    f_left = (col > 0).astype(F32)
    f_right = (col < lax.axis_size("dir") - 1).astype(F32)

    for j in range(4):
        for r in range(2):
            leaf_halo[r * 8 + j + 2] = before[j * 2 + r].astype(F32) * f_before
            leaf_halo[(r + 6) * 8 + j + 2] = after[j * 2 + r].astype(F32) * f_after
        for i in range(4):
            leaf_halo[(i + 2) * 8 + j + 2] = own[j * 4 + i].astype(F32)
    for part, flag, start in ((left, f_left, 0), (right, f_right, 6)):
        for c in range(2):
            for r in range(2):
                leaf_halo[r * 8 + start + c] = part[c * 2 + r].astype(F32) * (flag * f_before)
                leaf_halo[(r + 6) * 8 + start + c] = part[12 + c * 2 + r].astype(F32) * (
                    flag * f_after
                )
            for i in range(4):
                leaf_halo[(i + 2) * 8 + start + c] = part[4 + c * 4 + i].astype(F32) * flag
    for p in range(2):
        for q in range(2):
            for t in range(4):
                unit = (p * 2 + q) * 4 + t
                upper_halo[t, p * 6 + q + 2] = masked_unit(before[12 + unit], f_before)
                upper_halo[t, (p + 2) * 6 + q + 2] = own[32 + unit]
                upper_halo[t, (p + 4) * 6 + q + 2] = masked_unit(after[12 + unit], f_after)
                for part, flag, start in ((left, f_left, 0), (right, f_right, 4)):
                    upper_halo[t, p * 6 + q + start] = masked_unit(
                        part[22 + unit], flag * f_before
                    )
                    upper_halo[t, (p + 2) * 6 + q + start] = masked_unit(part[38 + unit], flag)
                    upper_halo[t, (p + 4) * 6 + q + start] = masked_unit(
                        part[54 + unit], flag * f_after
                    )

    def leaf_step(quad, carry):
        base = (quad // 2) * 16 + (quad % 2) * 2

        def keep(a, b, value):
            far[quad * 4 + a * 2 + b] = value

        translate(
            lambda r, c: leaf_halo[base + r * 8 + c],
            lambda part, dx, dy: trans_leaf[dx + 3, dy + 3, pl.ds(part, 1), :],
            keep,
        )
        return carry

    lax.fori_loop(0, 4, leaf_step, 0)

    sides = {}
    for j, part, flag in ((0, left, f_left), (3, right, f_right)):
        sides[j, -1] = masked_unit(part[16], flag * f_before)
        sides[j, 4] = masked_unit(part[21], flag * f_after)
        for i in range(4):
            sides[j, i] = masked_unit(part[17 + i], flag)
    for i in range(4):
        for j in range(4):
            value = near[i * 4 + j]
            if j in (0, 3):
                slots = [(3 if j else 0) + dx for dx in range(3)]
                value = value + near_sum(
                    [sides[j, i + dx] for dx in (-1, 0, 1)],
                    [rest[slot, 0, i] for slot in slots],
                    [rest[slot, 1, i] for slot in slots],
                )
            field[i * 4 + j] = value


def final_kernel(
    live,
    upper_halo,
    pieces,
    far,
    anterp,
    phase,
    near,
    rad,
    out_hbm,
    out,
    table,
    top,
    out_sems,
):
    for t in range(4):
        table[t] = pieces[pl.ds(t * 32, 32)].astype(F32).reshape(128, 128).T

    def top_step(t, carry):
        def keep(a, b, value):
            top[t, a * 2 + b] = value.astype(BF16).astype(F32)

        translate(
            lambda r, c: upper_halo[t, r * 6 + c].astype(F32),
            lambda part, dx, dy: table[t, pl.ds((part * 7 + dx + 3) * 8 + dy + 3, 1), :],
            keep,
        )
        return carry

    lax.fori_loop(0, 4, top_step, 0)

    rows = []
    for quad in range(4):
        for child in range(4):
            tiles = []
            for t in range(4):
                unit = top[t, quad]
                t_re, t_im = unit[0:8], unit[8:16]
                c = phase[child : child + 1, t * 128 : (t + 1) * 128]
                s = phase[4 + child : 5 + child, t * 128 : (t + 1) * 128]
                tiles.append(pair(c * t_re + s * t_im, c * t_im - s * t_re).astype(BF16))
            rows.append(jnp.concatenate(tiles, axis=1))
    back = dot_nt(jnp.concatenate(rows, axis=0), anterp[...])
    sent = []
    for i in range(4):
        for j in range(4):
            at = ((i // 2) * 2 + j // 2) * 4 + (i % 2) * 2 + j % 2
            total = (far[at] + back[at * 16 : at * 16 + 16]).astype(BF16)
            both = dot_nt(total, rad[:, i, j].reshape(256, 128))
            first, second = both[:, 0:128], both[:, 128:256]
            field = near[i * 4 + j] + pair(
                first[0:8] + second[8:16], first[8:16] - second[0:8]
            )
            on = live[i * 4 + j]
            out[0, i, j] = field[0:8] * on
            out[1, i, j] = field[8:16] * on
        sent.append(pltpu.make_async_copy(out.at[:, i], out_hbm.at[:, i], out_sems.at[i]))
        sent[-1].start()
    for copy in sent:
        copy.wait()


def unit_shape(count):
    return jax.ShapeDtypeStruct((count, 16, 128), BF16)


def shards(
    coeffs, counts, radiation, near_blocks, trans_leaf, interp, anterp, shift_angle, trans_top
):
    n_box = lax.axis_size("box")
    n_dir = lax.axis_size("dir")
    devices = n_box * n_dir
    outputs = (
        unit_shape(OWN),
        unit_shape(EDGE),
        unit_shape(EDGE),
        jax.ShapeDtypeStruct((8, 512), F32),
        jax.ShapeDtypeStruct((16, 8, 128), F32),
        jax.ShapeDtypeStruct((devices, 4, 128), F32),
    )
    own, to_after, to_before, phase, live, pieces = pl.pallas_call(
        leaf_kernel,
        out_shape=outputs,
        in_specs=[hbm()] * 6,
        out_specs=(hbm(),) * 6,
        scratch_shapes=[
            pltpu.SMEM((4, 4), jnp.int32),
            pltpu.VMEM((2, 4, 4, 8, 128), BF16),
            pltpu.VMEM((2, 4, 4, 128, 128), BF16),
            pltpu.VMEM((512, 128), BF16),
            pltpu.VMEM((4, 512), F32),
            pltpu.VMEM((2, 7, 4, 7), F32),
        ]
        + [pltpu.VMEM(out.shape, out.dtype) for out in outputs]
        + [
            pltpu.SemaphoreType.DMA((5,)),
            pltpu.SemaphoreType.DMA((4,)),
            pltpu.SemaphoreType.DMA((9,)),
        ],
        compiler_params=params(62),
        cost_estimate=cost(2),
        name="leaf",
    )(counts, coeffs, radiation, interp, shift_angle, trans_top.transpose(0, 1, 3, 2))
    forward = [(i, (i + 1) % n_box) for i in range(n_box)]
    backward = [((i + 1) % n_box, i) for i in range(n_box)]
    before = lax.ppermute(to_after, "box", forward)
    after = lax.ppermute(to_before, "box", backward)
    pieces = pl.pallas_call(
        pass_kernel,
        out_shape=jax.ShapeDtypeStruct((devices, 4, 128), F32),
        in_specs=[hbm()],
        out_specs=hbm(),
        input_output_aliases={0: 0},
        compiler_params=params(62),
        cost_estimate=cost(20),
        name="pass",
    )(pieces)
    gathered = lax.all_to_all(pieces, ("box", "dir"), split_axis=0, concat_axis=0, tiled=True)
    to_right, to_left = pl.pallas_call(
        pack_kernel,
        out_shape=(unit_shape(SIDE), unit_shape(SIDE)),
        in_specs=[vmem()] * 3,
        out_specs=(vmem(),) * 2,
        compiler_params=params(4),
        cost_estimate=cost(20),
        name="pack",
    )(own, before, after)
    left = lax.ppermute(to_right, "dir", [(i, (i + 1) % n_dir) for i in range(n_dir)])
    right = lax.ppermute(to_left, "dir", [((i + 1) % n_dir, i) for i in range(n_dir)])
    near, rest = pl.pallas_call(
        near_kernel,
        out_shape=(
            jax.ShapeDtypeStruct((16, 16, 128), F32),
            jax.ShapeDtypeStruct((6, 2, 4, 128, 128), BF16),
        ),
        in_specs=[vmem()] * 3 + [hbm()],
        out_specs=(vmem(),) * 2,
        scratch_shapes=[
            pltpu.VMEM((2, 4, 4, 9, 128, 128), BF16),
            pltpu.SemaphoreType.DMA((4, 7)),
            pltpu.SemaphoreType.DMA((6,)),
        ],
        compiler_params=params(48),
        cost_estimate=cost(4),
        name="near",
    )(own, before, after, near_blocks)
    far, upper_halo, near = pl.pallas_call(
        middle_kernel,
        out_shape=(
            jax.ShapeDtypeStruct((16, 16, 128), F32),
            jax.ShapeDtypeStruct((4, 36, 16, 128), BF16),
            jax.ShapeDtypeStruct((16, 16, 128), F32),
        ),
        in_specs=[vmem()] * 8,
        out_specs=(vmem(),) * 3,
        scratch_shapes=[pltpu.VMEM((64, 16, 128), F32)],
        compiler_params=params(48),
        cost_estimate=cost(2),
        name="middle",
    )(
        own,
        before,
        after,
        left,
        right,
        trans_leaf.transpose(1, 2, 0, 3),
        near,
        rest,
    )
    return pl.pallas_call(
        final_kernel,
        out_shape=jax.ShapeDtypeStruct((2, 4, 4, 8, 128), F32),
        in_specs=[vmem()] * 8,
        out_specs=hbm(),
        scratch_shapes=[
            pltpu.VMEM((2, 4, 4, 8, 128), F32),
            pltpu.VMEM((4, 128, 128), F32),
            pltpu.VMEM((4, 4, 16, 128), F32),
            pltpu.SemaphoreType.DMA((4,)),
        ],
        compiler_params=params(48),
        cost_estimate=cost(4),
        name="final",
    )(live, upper_halo, gathered, far, anterp, phase, near, radiation)


def solution(mesh):
    return jax.shard_map(
        shards,
        mesh=mesh,
        in_specs=(
            P(None, "box", "dir", None, None),
            P("box", "dir"),
            P(None, "box", "dir", None, None),
            P(None, "box", "dir", None, None, None),
            P(),
            P(),
            P(),
            P(),
            P(None, None, None, ("box", "dir")),
        ),
        out_specs=P(None, "box", "dir", None, None),
        check_vma=False,
    )
```

time: 32.5 us -> 29 us (0.89)
  Pallas kernels: 12.5 us -> 10.4 us
  waiting for transfers between devices: 3.72 us -> 3.01 us
  local copies, waits for them, and re-layouts: 0.7 us -> 0.02 us
    all_to_all x1, waiting for transfers between devices: 3.71 us -> 0.27 us  [shards(): lax.all_to_all(pieces, ('box', 'dir'), split_axis=0, concat_axis=0, tiled...]
    ppermute x1, waiting for transfers between devices: 0.01 us -> 2.14 us  [shards(): lax.ppermute(to_left, 'dir', [((i + 1) % n_dir, i) for i in range(n_dir)])]
    pallas_call x1, Pallas kernels: 3.93 us -> 1.83 us  [shards(): pl.pallas_call(final_kernel, out_shape=jax.ShapeDtypeStruct((2, 4, 4, 8,...]
    pallas_call x3 -> x4, Pallas kernels: 7.61 us -> 8.52 us  [the longest x1 4.62 us: shards(): pl.pallas_call(near_kernel, out_shape=(jax.ShapeDtypeStruct((16, 16, 128)...]
    pallas_call x1, Pallas kernels: 0.94 us -> 0.07 us  [shards(): pl.pallas_call(pack_kernel, out_shape=(unit_shape(SIDE), unit_shape(SIDE)...]
    unnamed x14 -> x12, local copies, waits for them, and re-layouts: 0.7 us -> 0.02 us
    ppermute x1, waiting for transfers between devices: 0.01 us -> 0.6 us  [shards(): lax.ppermute(to_right, 'dir', [(i, (i + 1) % n_dir) for i in range(n_dir)])]
  transfers between devices with their start and end apart: 5 -> 5, of which waited for: 1 -> 3; matrix products, arithmetic and copies ran while one was open for 0% -> 0% of each run, Pallas kernels for 19% -> 21%
where the time goes in v2:
time: 29 us; the launch traced here: 28.8 us
  starting transfers between devices  15.3 us (53%)
  Pallas kernels  10.4 us (36%)
  waiting for transfers between devices  3.01 us (10%)
    all_to_all x1, starting transfers between devices, shards(): lax.all_to_all(pieces, ('box', 'dir'), split_axis=0, concat_axis=0, tiled...  6.66 us
    pallas_call x1, Pallas kernels, shards(): pl.pallas_call(near_kernel, out_shape=(jax.ShapeDtypeStruct((16, 16, 128)...  4.62 us
    ppermute x1, starting transfers between devices, shards(): after = lax.ppermute(to_before, 'box', backward)  4.4 us
    pallas_call x1, Pallas kernels, shards(): pl.pallas_call(leaf_kernel, out_shape=outputs, in_specs=[hbm()] * 6, out_...  2.56 us
    ppermute x1, starting transfers between devices, shards(): before = lax.ppermute(to_after, 'box', forward)  2.53 us
    ppermute x1, waiting for transfers between devices, shards(): lax.ppermute(to_left, 'dir', [((i + 1) % n_dir, i) for i in range(n_dir)])  2.14 us
    pallas_call x1, Pallas kernels, shards(): pl.pallas_call(final_kernel, out_shape=jax.ShapeDtypeStruct((2, 4, 4, 8,...  1.83 us
    ppermute x1, starting transfers between devices, shards(): lax.ppermute(to_right, 'dir', [(i, (i + 1) % n_dir) for i in range(n_dir)])  1.65 us
  transfers between devices with their start and end apart: 5, of which 3 were waited for; matrix products, arithmetic and copies ran while one was open for 0% of the time, Pallas kernels for 21%

profile of v2, /device:TPU:1, one launch (start us, length us, event | category | flops | bytes accessed | tf_op | source)
XLA Modules:
  0.0 28.8 jit_solution(17031014747157951251)
XLA Ops:
  0.0 2.6 %leaf.1 = (bf16[48,16,128]{2,1,0:T(8,128)(2,1)}, bf16[28,16,128]{2,1,0:T(8,128)(2,1)}, bf16[28,16,128]{2,1,0:T(8,128)(2,1)}, f32[8,512]{1,0:T(8,128)}, f32[16,8,128]{2,1,0:T(8,128)}, /*index=5*/f32[128,4,128]{2,1,0:T(4,128)}) custom-call(s32[4,4]{1,0:T(4,128)} %counts_hbm.1, bf16[2,4,4,8,128]{4,3,2,1,0:T(8,128)(2,1)} %coeffs_hbm.1, ...), custom_call_target="tpu_custom_call" | custom-call | flops 2000000000 | bytes 2097152 | tf_op jit(solution)/shard_map/leaf/pallas_call | solution.py:430
  2.6 2.5 %collective-permute-start = (bf16[28,16,128]{2,1,0:T(8,128)(2,1)}, bf16[28,16,128]{2,1,0:T(8,128)(2,1)S(1)}, u32[]{:S(2)}, u32[]{:S(2)}) collective-permute-start(bf16[28,16,128]{2,1,0:T(8,128)(2,1)} %get-tuple-element.20), channel_id=1, source_target_pairs={{0,8},{8,16},{16,24},{24,32},{32,40},{40,48},{48,56},{56,64},{64,7... | collective-permute-start | bytes 344072 | tf_op jit(solution)/shard_map/ppermute | solution.py:455
  5.1 4.4 %collective-permute-start.1 = (bf16[28,16,128]{2,1,0:T(8,128)(2,1)}, bf16[28,16,128]{2,1,0:T(8,128)(2,1)S(1)}, u32[]{:S(2)}, u32[]{:S(2)}) collective-permute-start(bf16[28,16,128]{2,1,0:T(8,128)(2,1)} %get-tuple-element.21), channel_id=1, source_target_pairs={{8,0},{16,8},{24,16},{32,24},{40,32},{48,40},{56,48},{64,56},{72,6... | collective-permute-start | bytes 344072 | tf_op jit(solution)/shard_map/ppermute | solution.py:456
  9.5 0.0 copy-start.3
  9.5 6.7 %all-to-all-start = ((f32[128,4,128]{2,1,0:T(4,128)}), f32[128,4,128]{2,1,0:T(4,128)S(1)}, u32[]{:S(2)}, u32[]{:S(2)}) async-start(f32[128,4,128]{2,1,0:T(4,128)} %pass.1), calls=%async_computation | async-start | bytes 524288 | tf_op jit(solution)/shard_map/all_to_all | solution.py:467
  16.2 0.0 collective-permute-done.before
  16.2 0.0 collective-permute-done.1.after
  16.2 0.0 copy-done.3
  16.2 0.1 pack.1
  16.3 0.0 copy-start.2
  16.3 1.6 %collective-permute-start.2 = (bf16[70,16,128]{2,1,0:T(8,128)(2,1)S(1)}, bf16[70,16,128]{2,1,0:T(8,128)(2,1)S(1)}, u32[]{:S(2)}, u32[]{:S(2)}) collective-permute-start(bf16[70,16,128]{2,1,0:T(8,128)(2,1)S(1)} %get-tuple-element.22), channel_id=1, source_target_pairs={{0,1},{1,2},{2,3},{3,4},{4,5},{5,6},{6,7},{7,0},{8,9},{9,10},{10,1... | collective-permute-start | bytes 860168 | tf_op jit(solution)/shard_map/ppermute | solution.py:477
  17.9 0.0 copy-start
  17.9 0.0 copy-start.1
  17.9 0.0 copy-start.4
  17.9 0.0 copy-start.5
  17.9 0.0 collective-permute-start.3
  18.0 4.6 %near.1 = (f32[16,16,128]{2,1,0:T(8,128)S(1)}, bf16[6,2,4,128,128]{4,3,2,1,0:T(8,128)(2,1)S(1)}) custom-call(bf16[48,16,128]{2,1,0:T(8,128)(2,1)S(1)} %copy-done.3, bf16[28,16,128]{2,1,0:T(8,128)(2,1)S(1)} %collective-permute-done.before, bf16[28,16,128]{2,1,0:T(8,128)(2,1)S(1)} %collective-permute-done.1.after, bf16[2,4,4,9,128,128]{5,4,3,2,1,0:T(8,128)(2,1)} %blocks.1), custom_call_target="tpu_custom_call" | custom-call | flops 4000000000 | bytes 4194304 | tf_op jit(solution)/shard_map/near/pallas_call | solution.py:479
  22.6 0.6 %collective-permute-done.2.left = bf16[70,16,128]{2,1,0:T(8,128)(2,1)S(1)} collective-permute-done((bf16[70,16,128]{2,1,0:T(8,128)(2,1)S(1)}, bf16[70,16,128]{2,1,0:T(8,128)(2,1)S(1)}, u32[]{:S(2)}, u32[]{:S(2)}) %collective-permute-start.2) | collective-permute-done | bytes 286752 | tf_op jit(solution)/shard_map/ppermute | solution.py:477
  23.2 2.1 %collective-permute-done.3.right = bf16[70,16,128]{2,1,0:T(8,128)(2,1)S(1)} collective-permute-done((bf16[70,16,128]{2,1,0:T(8,128)(2,1)S(1)}, bf16[70,16,128]{2,1,0:T(8,128)(2,1)S(1)}, u32[]{:S(2)}, u32[]{:S(2)}) %collective-permute-start.3) | collective-permute-done | bytes 286752 | tf_op jit(solution)/shard_map/ppermute | solution.py:478
  25.3 0.0 copy-done.2
  25.3 1.3 %middle.1 = (f32[16,16,128]{2,1,0:T(8,128)S(1)}, bf16[4,36,16,128]{3,2,1,0:T(8,128)(2,1)S(1)}, f32[16,16,128]{2,1,0:T(8,128)S(1)}) custom-call(bf16[48,16,128]{2,1,0:T(8,128)(2,1)S(1)} %copy-done.3, bf16[28,16,128]{2,1,0:T(8,128)(2,1)S(1)} %collective-permute-done.before, bf16[28,16,128]{2,1,0:T(8,128)(2,1)S(1)} %collective-permute-done.1.after, ...), custom_call_target="tpu_custom_call" | custom-call | flops 2000000000 | bytes 2097152 | tf_op jit(solution)/shard_map/middle/pallas_call | solution.py:496
  26.7 0.3 all-to-all-done.pieces
  26.9 0.0 copy-done
  26.9 0.0 copy-done.1
  26.9 0.0 copy-done.4
  27.0 0.0 copy-done.5
  27.0 1.8 %final.1 = f32[2,4,4,8,128]{4,3,2,1,0:T(8,128)} custom-call(f32[16,8,128]{2,1,0:T(8,128)S(1)} %copy-done.4, bf16[4,36,16,128]{3,2,1,0:T(8,128)(2,1)S(1)} %get-tuple-element.26.upper_halo, f32[128,4,128]{2,1,0:T(4,128)S(1)} %all-to-all-done.pieces, f32[16,16,128]{2,1,0:T(8,128)S(1)} %get-tuple-element.28.far, bf16[128,512]{1,0:T(8,128)(2,1)S(1)} %copy-done.1, ...), custom_call_target="tpu_custom_call" | custom-call | flops 4000000000 | bytes 4194304 | tf_op jit(solution)/shard_map/final/pallas_call | solution.py:519
  (1 shorter events, 0.0 us)
Async XLA Ops:
  2.6 13.6 %collective-permute-start = (bf16[28,16,128]{2,1,0:T(8,128)(2,1)}, bf16[28,16,128]{2,1,0:T(8,128)(2,1)S(1)}, u32[]{:S(2)}, u32[]{:S(2)}) collective-permute-start(bf16[28,16,128]{2,1,0:T(8,128)(2,1)} %get-tuple-element.20), channel_id=1, source_target_pairs={{0,8},{8,16},{16,24},{24,32},{32,40},{40,48},{48,56},{56,64},{64,7... | collective-permute-start | bytes 344072 | tf_op jit(solution)/shard_map/ppermute | solution.py:455
  5.1 11.1 %collective-permute-start.1 = (bf16[28,16,128]{2,1,0:T(8,128)(2,1)}, bf16[28,16,128]{2,1,0:T(8,128)(2,1)S(1)}, u32[]{:S(2)}, u32[]{:S(2)}) collective-permute-start(bf16[28,16,128]{2,1,0:T(8,128)(2,1)} %get-tuple-element.21), channel_id=1, source_target_pairs={{8,0},{16,8},{24,16},{32,24},{40,32},{48,40},{56,48},{64,56},{72,6... | collective-permute-start | bytes 344072 | tf_op jit(solution)/shard_map/ppermute | solution.py:456
  9.5 6.7 %copy-start.3 = (bf16[48,16,128]{2,1,0:T(8,128)(2,1)S(1)}, bf16[48,16,128]{2,1,0:T(8,128)(2,1)}, u32[]{:S(2)}) copy-start(bf16[48,16,128]{2,1,0:T(8,128)(2,1)} %get-tuple-element.19.own) | copy-start | bytes 589828
  9.5 17.4 %all-to-all-start = ((f32[128,4,128]{2,1,0:T(4,128)}), f32[128,4,128]{2,1,0:T(4,128)S(1)}, u32[]{:S(2)}, u32[]{:S(2)}) async-start(f32[128,4,128]{2,1,0:T(4,128)} %pass.1), calls=%async_computation | async-start | bytes 524288 | tf_op jit(solution)/shard_map/all_to_all | solution.py:467
  16.3 9.1 %copy-start.2 = (f32[2,7,7,128]{3,0,2,1:T(2,128)S(1)}, f32[2,7,7,128]{3,0,2,1:T(2,128)}, u32[]{:S(2)}) copy-start(f32[2,7,7,128]{3,0,2,1:T(2,128)} %param.13) | copy-start | bytes 150532
  16.3 6.9 %collective-permute-start.2 = (bf16[70,16,128]{2,1,0:T(8,128)(2,1)S(1)}, bf16[70,16,128]{2,1,0:T(8,128)(2,1)S(1)}, u32[]{:S(2)}, u32[]{:S(2)}) collective-permute-start(bf16[70,16,128]{2,1,0:T(8,128)(2,1)S(1)} %get-tuple-element.22), channel_id=1, source_target_pairs={{0,1},{1,2},{2,3},{3,4},{4,5},{5,6},{6,7},{7,0},{8,9},{9,10},{10,1... | collective-permute-start | bytes 860168 | tf_op jit(solution)/shard_map/ppermute | solution.py:477
  17.9 9.0 %copy-start = (bf16[2,4,4,128,128]{4,3,2,1,0:T(8,128)(2,1)S(1)}, bf16[2,4,4,128,128]{4,3,2,1,0:T(8,128)(2,1)}, u32[]{:S(2)}) copy-start(bf16[2,4,4,128,128]{4,3,2,1,0:T(8,128)(2,1)} %rad.1) | copy-start | bytes 3145732
  17.9 9.0 %copy-start.1 = (bf16[128,512]{1,0:T(8,128)(2,1)S(1)}, bf16[128,512]{1,0:T(8,128)(2,1)}, u32[]{:S(2)}) copy-start(bf16[128,512]{1,0:T(8,128)(2,1)} %anterp.1) | copy-start | bytes 393220
  17.9 9.0 %copy-start.4 = (f32[16,8,128]{2,1,0:T(8,128)S(1)}, f32[16,8,128]{2,1,0:T(8,128)}, u32[]{:S(2)}) copy-start(f32[16,8,128]{2,1,0:T(8,128)} %get-tuple-element.18.live) | copy-start | bytes 196612
  17.9 9.0 %copy-start.5 = (f32[8,512]{1,0:T(8,128)S(1)}, f32[8,512]{1,0:T(8,128)}, u32[]{:S(2)}) copy-start(f32[8,512]{1,0:T(8,128)} %get-tuple-element.29.phase) | copy-start | bytes 49156
  17.9 7.4 %collective-permute-start.3 = (bf16[70,16,128]{2,1,0:T(8,128)(2,1)S(1)}, bf16[70,16,128]{2,1,0:T(8,128)(2,1)S(1)}, u32[]{:S(2)}, u32[]{:S(2)}) collective-permute-start(bf16[70,16,128]{2,1,0:T(8,128)(2,1)S(1)} %get-tuple-element.23), channel_id=1, source_target_pairs={{1,0},{2,1},{3,2},{4,3},{5,4},{6,5},{7,6},{0,7},{9,8},{10,9},{11,1... | collective-permute-start | bytes 860168 | tf_op jit(solution)/shard_map/ppermute | solution.py:478

commit v3 on v2

--- a/solution.py
+++ b/solution.py
@@ -81,12 +81,12 @@
         copy.start()
         sent.append(copy)
 
-    pieces[0] = jnp.zeros((4, 128), F32)
+    pieces[0] = jnp.zeros((4, 128), BF16)
     table_in.wait()
     for part in range(2):
         for dx in range(7):
             at = (part * 7 + dx) * 8
-            pieces[0, :, at : at + 7] = table[part, dx]
+            pieces[0, :, at : at + 7] = table[part, dx].astype(BF16)
     pieces[...] = jnp.broadcast_to(pieces[0:1], pieces.shape)
     send(pieces, pieces_hbm)
     angle_in.wait()
@@ -182,6 +182,16 @@
     return pair(first[0:8] - second[8:16], first[8:16] + second[0:8])
 
 
+def border_flags():
+    box, col = lax.axis_index("box"), lax.axis_index("dir")
+    return (
+        (box > 0).astype(F32),
+        (box < lax.axis_size("box") - 1).astype(F32),
+        (col > 0).astype(F32),
+        (col < lax.axis_size("dir") - 1).astype(F32),
+    )
+
+
 def masked_unit(unit, flag):
     return (unit.astype(F32) * flag).astype(BF16)
 
@@ -190,7 +200,9 @@
     return [dy for dy in (-1, 0, 1) if 0 <= j + dy < 4]
 
 
-def near_kernel(own, before, after, blocks, out, rest, held, sems, rest_sems):
+def near_kernel(
+    own, before, after, trans_leaf, blocks, out, rest, far, held, leaf_halo, sems, rest_sems
+):
     copies = []
     for i in range(4):
         group = [pltpu.make_async_copy(blocks.at[:, i, 1:3], held.at[:, i, 1:3], sems.at[i, 0])]
@@ -217,15 +229,34 @@
             )
     for copy in rest_copies:
         copy.start()
-    here = lax.axis_index("box")
-    has_before = (here > 0).astype(F32)
-    has_after = (here < lax.axis_size("box") - 1).astype(F32)
+    has_before, has_after, _, _ = border_flags()
     rows = {}
     for j in range(4):
         rows[-1, j] = (before[8 + j].astype(F32) * has_before).astype(BF16)
         rows[4, j] = (after[8 + j].astype(F32) * has_after).astype(BF16)
         for i in range(4):
             rows[i, j] = own[16 + j * 4 + i]
+    for j in range(4):
+        for r in range(2):
+            leaf_halo[r * 4 + j] = before[j * 2 + r].astype(F32) * has_before
+            leaf_halo[(r + 6) * 4 + j] = after[j * 2 + r].astype(F32) * has_after
+        for i in range(4):
+            leaf_halo[(i + 2) * 4 + j] = own[j * 4 + i].astype(F32)
+
+    def far_step(big_i, carry):
+        for big_j in range(2):
+            first = 2 - 2 * big_j
+            total = translate(
+                lambda r, c: leaf_halo[(big_i * 2 + r) * 4 + c - first],
+                lambda part, dx, dy: trans_leaf[dx + 3, dy + 3, pl.ds(part, 1), :],
+                {},
+                range(first, first + 4),
+            )
+            for a, b in CHILDREN:
+                far[(big_i * 2 + big_j) * 4 + a * 2 + b] = pair(*total[a, b])
+        return carry
+
+    lax.fori_loop(0, 2, far_step, 0)
     for i in range(4):
         for copy in copies[i]:
             copy.wait()
@@ -240,26 +271,33 @@
         copy.wait()
 
 
-def translate(source, coef, keep):
-    total = {}
-    for r in range(6):
-        for c in range(6):
-            unit = source(r, c)
-            s_re, s_im = unit[0:8], unit[8:16]
+def translate(source, coef, start, cols):
+    total = dict(start)
+    for dx in range(-3, 4):
+        for dy in range(-3, 4):
+            if max(abs(dx), abs(dy)) < 2:
+                continue
+            k_re = k_im = None
             for a in range(2):
                 for b in range(2):
-                    dx, dy = r - 2 - a, c - 2 - b
-                    if max(abs(dx), abs(dy)) < 2:
+                    r, c = dx + 2 + a, dy + 2 + b
+                    if not 0 <= r < 6 or c not in cols:
                         continue
-                    k_re, k_im = coef(0, dx, dy), coef(1, dx, dy)
+                    if k_re is None:
+                        k_re = jnp.broadcast_to(coef(0, dx, dy), (8, 128))
+                        k_im = jnp.broadcast_to(coef(1, dx, dy), (8, 128))
+                    unit = source(r, c)
+                    s_re, s_im = unit[0:8], unit[8:16]
                     t_re = k_re * s_re - k_im * s_im
                     t_im = k_re * s_im + k_im * s_re
                     if (a, b) in total:
                         old_re, old_im = total[a, b]
                         t_re, t_im = old_re + t_re, old_im + t_im
                     total[a, b] = (t_re, t_im)
-    for (a, b), (t_re, t_im) in total.items():
-        keep(a, b, pair(t_re, t_im))
+    return total
+
+
+CHILDREN = [(a, b) for a in range(2) for b in range(2)]
 
 
 def middle_kernel(
@@ -271,62 +309,57 @@
     trans_leaf,
     near,
     rest,
+    far_own,
     far,
     upper_halo,
     field,
     leaf_halo,
 ):
-    box, col = lax.axis_index("box"), lax.axis_index("dir")
-    f_before = (box > 0).astype(F32)
-    f_after = (box < lax.axis_size("box") - 1).astype(F32)
-    f_left = (col > 0).astype(F32)
-    f_right = (col < lax.axis_size("dir") - 1).astype(F32)
-
-    for j in range(4):
-        for r in range(2):
-            leaf_halo[r * 8 + j + 2] = before[j * 2 + r].astype(F32) * f_before
-            leaf_halo[(r + 6) * 8 + j + 2] = after[j * 2 + r].astype(F32) * f_after
-        for i in range(4):
-            leaf_halo[(i + 2) * 8 + j + 2] = own[j * 4 + i].astype(F32)
-    for part, flag, start in ((left, f_left, 0), (right, f_right, 6)):
+    f_before, f_after, f_left, f_right = border_flags()
+    for side, (part, flag) in enumerate(((left, f_left), (right, f_right))):
         for c in range(2):
             for r in range(2):
-                leaf_halo[r * 8 + start + c] = part[c * 2 + r].astype(F32) * (flag * f_before)
-                leaf_halo[(r + 6) * 8 + start + c] = part[12 + c * 2 + r].astype(F32) * (
+                leaf_halo[side, r * 2 + c] = part[c * 2 + r].astype(F32) * (flag * f_before)
+                leaf_halo[side, (r + 6) * 2 + c] = part[12 + c * 2 + r].astype(F32) * (
                     flag * f_after
                 )
             for i in range(4):
-                leaf_halo[(i + 2) * 8 + start + c] = part[4 + c * 4 + i].astype(F32) * flag
+                leaf_halo[side, (i + 2) * 2 + c] = part[4 + c * 4 + i].astype(F32) * flag
     for p in range(2):
         for q in range(2):
             for t in range(4):
                 unit = (p * 2 + q) * 4 + t
-                upper_halo[t, p * 6 + q + 2] = masked_unit(before[12 + unit], f_before)
-                upper_halo[t, (p + 2) * 6 + q + 2] = own[32 + unit]
-                upper_halo[t, (p + 4) * 6 + q + 2] = masked_unit(after[12 + unit], f_after)
+                upper_halo[t, p * 6 + q + 2] = before[12 + unit].astype(F32) * f_before
+                upper_halo[t, (p + 2) * 6 + q + 2] = own[32 + unit].astype(F32)
+                upper_halo[t, (p + 4) * 6 + q + 2] = after[12 + unit].astype(F32) * f_after
                 for part, flag, start in ((left, f_left, 0), (right, f_right, 4)):
-                    upper_halo[t, p * 6 + q + start] = masked_unit(
-                        part[22 + unit], flag * f_before
+                    upper_halo[t, p * 6 + q + start] = part[22 + unit].astype(F32) * (
+                        flag * f_before
                     )
-                    upper_halo[t, (p + 2) * 6 + q + start] = masked_unit(part[38 + unit], flag)
-                    upper_halo[t, (p + 4) * 6 + q + start] = masked_unit(
-                        part[54 + unit], flag * f_after
+                    upper_halo[t, (p + 2) * 6 + q + start] = part[38 + unit].astype(F32) * flag
+                    upper_halo[t, (p + 4) * 6 + q + start] = part[54 + unit].astype(F32) * (
+                        flag * f_after
                     )
 
-    def leaf_step(quad, carry):
-        base = (quad // 2) * 16 + (quad % 2) * 2
-
-        def keep(a, b, value):
-            far[quad * 4 + a * 2 + b] = value
-
-        translate(
-            lambda r, c: leaf_halo[base + r * 8 + c],
-            lambda part, dx, dy: trans_leaf[dx + 3, dy + 3, pl.ds(part, 1), :],
-            keep,
-        )
+    def far_step(big_i, carry):
+        for big_j in range(2):
+            first = 4 * big_j
+            at = (big_i * 2 + big_j) * 4
+            start = {}
+            for a, b in CHILDREN:
+                unit = far_own[at + a * 2 + b]
+                start[a, b] = (unit[0:8], unit[8:16])
+            total = translate(
+                lambda r, c: leaf_halo[big_j, (big_i * 2 + r) * 2 + c - first],
+                lambda part, dx, dy: trans_leaf[dx + 3, dy + 3, pl.ds(part, 1), :],
+                start,
+                range(first, first + 2),
+            )
+            for a, b in CHILDREN:
+                far[at + a * 2 + b] = pair(*total[a, b])
         return carry
 
-    lax.fori_loop(0, 4, leaf_step, 0)
+    lax.fori_loop(0, 2, far_step, 0)
 
     sides = {}
     for j, part, flag in ((0, left, f_left), (3, right, f_right)):
@@ -366,14 +399,14 @@
         table[t] = pieces[pl.ds(t * 32, 32)].astype(F32).reshape(128, 128).T
 
     def top_step(t, carry):
-        def keep(a, b, value):
-            top[t, a * 2 + b] = value.astype(BF16).astype(F32)
-
-        translate(
-            lambda r, c: upper_halo[t, r * 6 + c].astype(F32),
+        total = translate(
+            lambda r, c: upper_halo[t, r * 6 + c],
             lambda part, dx, dy: table[t, pl.ds((part * 7 + dx + 3) * 8 + dy + 3, 1), :],
-            keep,
+            {},
+            range(6),
         )
+        for a, b in CHILDREN:
+            top[t, a * 2 + b] = pair(*total[a, b]).astype(BF16).astype(F32)
         return carry
 
     lax.fori_loop(0, 4, top_step, 0)
@@ -425,7 +458,7 @@
         unit_shape(EDGE),
         jax.ShapeDtypeStruct((8, 512), F32),
         jax.ShapeDtypeStruct((16, 8, 128), F32),
-        jax.ShapeDtypeStruct((devices, 4, 128), F32),
+        jax.ShapeDtypeStruct((devices, 4, 128), BF16),
     )
     own, to_after, to_before, phase, live, pieces = pl.pallas_call(
         leaf_kernel,
@@ -456,7 +489,7 @@
     after = lax.ppermute(to_before, "box", backward)
     pieces = pl.pallas_call(
         pass_kernel,
-        out_shape=jax.ShapeDtypeStruct((devices, 4, 128), F32),
+        out_shape=jax.ShapeDtypeStruct((devices, 4, 128), BF16),
         in_specs=[hbm()],
         out_specs=hbm(),
         input_output_aliases={0: 0},
@@ -476,46 +509,40 @@
     )(own, before, after)
     left = lax.ppermute(to_right, "dir", [(i, (i + 1) % n_dir) for i in range(n_dir)])
     right = lax.ppermute(to_left, "dir", [((i + 1) % n_dir, i) for i in range(n_dir)])
-    near, rest = pl.pallas_call(
+    by_offset = trans_leaf.transpose(1, 2, 0, 3)
+    near, rest, far = pl.pallas_call(
         near_kernel,
         out_shape=(
             jax.ShapeDtypeStruct((16, 16, 128), F32),
             jax.ShapeDtypeStruct((6, 2, 4, 128, 128), BF16),
+            jax.ShapeDtypeStruct((16, 16, 128), F32),
         ),
-        in_specs=[vmem()] * 3 + [hbm()],
-        out_specs=(vmem(),) * 2,
+        in_specs=[vmem()] * 4 + [hbm()],
+        out_specs=(vmem(),) * 3,
         scratch_shapes=[
             pltpu.VMEM((2, 4, 4, 9, 128, 128), BF16),
+            pltpu.VMEM((32, 16, 128), F32),
             pltpu.SemaphoreType.DMA((4, 7)),
             pltpu.SemaphoreType.DMA((6,)),
         ],
         compiler_params=params(48),
         cost_estimate=cost(4),
         name="near",
-    )(own, before, after, near_blocks)
+    )(own, before, after, by_offset, near_blocks)
     far, upper_halo, near = pl.pallas_call(
         middle_kernel,
         out_shape=(
             jax.ShapeDtypeStruct((16, 16, 128), F32),
-            jax.ShapeDtypeStruct((4, 36, 16, 128), BF16),
+            jax.ShapeDtypeStruct((4, 36, 16, 128), F32),
             jax.ShapeDtypeStruct((16, 16, 128), F32),
         ),
-        in_specs=[vmem()] * 8,
+        in_specs=[vmem()] * 9,
         out_specs=(vmem(),) * 3,
-        scratch_shapes=[pltpu.VMEM((64, 16, 128), F32)],
+        scratch_shapes=[pltpu.VMEM((2, 16, 16, 128), F32)],
         compiler_params=params(48),
         cost_estimate=cost(2),
         name="middle",
-    )(
-        own,
-        before,
-        after,
-        left,
-        right,
-        trans_leaf.transpose(1, 2, 0, 3),
-        near,
-        rest,
-    )
+    )(own, before, after, left, right, by_offset, near, rest, far)
     return pl.pallas_call(
         final_kernel,
         out_shape=jax.ShapeDtypeStruct((2, 4, 4, 8, 128), F32),

time: 29 us -> 28.1 us (0.969)
  Pallas kernels: 10.4 us -> 9.88 us
  waiting for transfers between devices: 3.01 us -> 2.69 us
    ppermute x1, waiting for transfers between devices: 0.6 us -> 0.01 us  [shards(): lax.ppermute(to_right, 'dir', [(i, (i + 1) % n_dir) for i in range(n_dir)])]
    pallas_call x1, Pallas kernels: 1.33 us -> 0.94 us  [shards(): pl.pallas_call(middle_kernel, out_shape=(jax.ShapeDtypeStruct((16, 16, 12...]
    all_to_all x1, waiting for transfers between devices: 0.27 us -> 0.57 us  [shards(): lax.all_to_all(pieces, ('box', 'dir'), split_axis=0, concat_axis=0, tiled...]
  transfers between devices with their start and end apart: 5 -> 5, of which waited for: 3 -> 2; matrix products, arithmetic and copies ran while one was open for 0% -> 0% of each run, Pallas kernels for 21% -> 20%
where the time goes in v3:
time: 28.1 us; the launch traced here: 27.9 us
  starting transfers between devices  15.2 us (54%)
  Pallas kernels  9.88 us (35%)
  waiting for transfers between devices  2.69 us (10%)
    all_to_all x1, starting transfers between devices, shards(): lax.all_to_all(pieces, ('box', 'dir'), split_axis=0, concat_axis=0, tiled...  6.66 us
    pallas_call x1, Pallas kernels, shards(): pl.pallas_call(near_kernel, out_shape=(jax.ShapeDtypeStruct((16, 16, 128)...  4.53 us
    ppermute x1, starting transfers between devices, shards(): after = lax.ppermute(to_before, 'box', backward)  4.4 us
    pallas_call x1, Pallas kernels, shards(): pl.pallas_call(leaf_kernel, out_shape=outputs, in_specs=[hbm()] * 6, out_...  2.56 us
    ppermute x1, starting transfers between devices, shards(): before = lax.ppermute(to_after, 'box', forward)  2.53 us
    ppermute x1, waiting for transfers between devices, shards(): lax.ppermute(to_left, 'dir', [((i + 1) % n_dir, i) for i in range(n_dir)])  2.11 us
    pallas_call x1, Pallas kernels, shards(): pl.pallas_call(final_kernel, out_shape=jax.ShapeDtypeStruct((2, 4, 4, 8,...  1.79 us
    ppermute x1, starting transfers between devices, shards(): lax.ppermute(to_right, 'dir', [(i, (i + 1) % n_dir) for i in range(n_dir)])  1.65 us
  transfers between devices with their start and end apart: 5, of which 2 were waited for; matrix products, arithmetic and copies ran while one was open for 0% of the time, Pallas kernels for 20%

profile of v3, /device:TPU:1, one launch (start us, length us, event | category | flops | bytes accessed | tf_op | source)
XLA Modules:
  0.0 27.9 jit_solution(4914521503642583455)
XLA Ops:
  0.0 2.6 %leaf.1 = (bf16[48,16,128]{2,1,0:T(8,128)(2,1)}, bf16[28,16,128]{2,1,0:T(8,128)(2,1)}, bf16[28,16,128]{2,1,0:T(8,128)(2,1)}, f32[8,512]{1,0:T(8,128)}, f32[16,8,...) custom-call(s32[4,4]{1,0:T(4,128)} %counts_hbm.1, bf16[2,4,4,8,128]{4,3,2,1,0:T(8,128)(2,1)} %coeffs_hbm.1, ...), custom_call_target="tpu_custom_call" | custom-call | flops 2000000000 | bytes 2097152 | tf_op jit(solution)/shard_map/leaf/pallas_call | solution.py:463
  2.6 2.5 %collective-permute-start = (bf16[28,16,128]{2,1,0:T(8,128)(2,1)}, bf16[28,16,128]{2,1,0:T(8,128)(2,1)S(1)}, u32[]{:S(2)}, u32[]{:S(2)}) collective-permute-start(bf16[28,16,128]{2,1,0:T(8,128)(2,1)} %get-tuple-element.21), channel_id=1, source_target_pairs={{0,8},{8,16},{16,24},{24,32},{32,40},{40,48},{48,56},{56,64},{64,7... | collective-permute-start | bytes 344072 | tf_op jit(solution)/shard_map/ppermute | solution.py:488
  5.1 4.4 %collective-permute-start.1 = (bf16[28,16,128]{2,1,0:T(8,128)(2,1)}, bf16[28,16,128]{2,1,0:T(8,128)(2,1)S(1)}, u32[]{:S(2)}, u32[]{:S(2)}) collective-permute-start(bf16[28,16,128]{2,1,0:T(8,128)(2,1)} %get-tuple-element.22), channel_id=1, source_target_pairs={{8,0},{16,8},{24,16},{32,24},{40,32},{48,40},{56,48},{64,56},{72,6... | collective-permute-start | bytes 344072 | tf_op jit(solution)/shard_map/ppermute | solution.py:489
  9.5 0.0 copy-start.3
  9.5 6.7 %all-to-all-start = ((bf16[128,4,128]{2,1,0:T(4,128)(2,1)}), bf16[128,4,128]{2,1,0:T(4,128)(2,1)S(1)}, u32[]{:S(2)}, u32[]{:S(2)}) async-start(bf16[128,4,128]{2,1,0:T(4,128)(2,1)} %pass.1), calls=%async_computation | async-start | bytes 262144 | tf_op jit(solution)/shard_map/all_to_all | solution.py:500
  16.2 0.0 collective-permute-done.before
  16.2 0.0 collective-permute-done.1.after
  16.2 0.0 copy-done.3
  16.2 0.0 copy-start.2
  16.2 0.1 pack.1
  16.3 1.6 %collective-permute-start.2 = (bf16[70,16,128]{2,1,0:T(8,128)(2,1)S(1)}, bf16[70,16,128]{2,1,0:T(8,128)(2,1)S(1)}, u32[]{:S(2)}, u32[]{:S(2)}) collective-permute-start(bf16[70,16,128]{2,1,0:T(8,128)(2,1)S(1)} %get-tuple-element.23), channel_id=1, source_target_pairs={{0,1},{1,2},{2,3},{3,4},{4,5},{5,6},{6,7},{7,0},{8,9},{9,10},{10,1... | collective-permute-start | bytes 860168 | tf_op jit(solution)/shard_map/ppermute | solution.py:510
  17.9 0.0 collective-permute-start.3
  17.9 0.0 copy-done.2
  17.9 4.5 %near.1 = (f32[16,16,128]{2,1,0:T(8,128)S(1)}, bf16[6,2,4,128,128]{4,3,2,1,0:T(8,128)(2,1)S(1)}, f32[16,16,128]{2,1,0:T(8,128)S(1)}) custom-call(bf16[48,16,128]{2,1,0:T(8,128)(2,1)S(1)} %copy-done.3, bf16[28,16,128]{2,1,0:T(8,128)(2,1)S(1)} %collective-permute-done.before, bf16[28,16,128]{2,1,0:T(8,128)(2,1)S(1)} %collective-permute-done.1.after, ...), custom_call_target="tpu_custom_call" | custom-call | flops 4000000000 | bytes 4194304 | tf_op jit(solution)/shard_map/near/pallas_call | solution.py:513
  22.5 0.0 collective-permute-done.2.left
  22.5 2.1 %collective-permute-done.3.right = bf16[70,16,128]{2,1,0:T(8,128)(2,1)S(1)} collective-permute-done((bf16[70,16,128]{2,1,0:T(8,128)(2,1)S(1)}, bf16[70,16,128]{2,1,0:T(8,128)(2,1)S(1)}, u32[]{:S(2)}, u32[]{:S(2)}) %collective-permute-start.3) | collective-permute-done | bytes 286752 | tf_op jit(solution)/shard_map/ppermute | solution.py:511
  24.6 0.0 copy-start
  24.6 0.0 copy-start.1
  24.6 0.0 copy-start.4
  24.6 0.0 copy-start.5
  24.6 0.9 %middle.1 = (f32[16,16,128]{2,1,0:T(8,128)S(1)}, f32[4,36,16,128]{3,2,1,0:T(8,128)S(1)}, f32[16,16,128]{2,1,0:T(8,128)S(1)}) custom-call(bf16[48,16,128]{2,1,0:T(8,128)(2,1)S(1)} %copy-done.3, bf16[28,16,128]{2,1,0:T(8,128)(2,1)S(1)} %collective-permute-done.before, bf16[28,16,128]{2,1,0:T(8,128)(2,1)S(1)} %collective-permute-done.1.after, ...), custom_call_target="tpu_custom_call" | custom-call | flops 2000000000 | bytes 2097152 | tf_op jit(solution)/shard_map/middle/pallas_call | solution.py:532
  25.5 0.6 %all-to-all-done.pieces = bf16[128,4,128]{2,1,0:T(4,128)(2,1)S(1)} async-done(((bf16[128,4,128]{2,1,0:T(4,128)(2,1)}), bf16[128,4,128]{2,1,0:T(4,128)(2,1)S(1)}, u32[]{:S(2)}, u32[]{:S(2)}) %all-to-all-start) | async-done | bytes 131104 | tf_op jit(solution)/shard_map/all_to_all | solution.py:500
  26.1 0.0 copy-done
  26.1 0.0 copy-done.1
  26.1 0.0 copy-done.4
  26.1 0.0 copy-done.5
  26.1 1.8 %final.1 = f32[2,4,4,8,128]{4,3,2,1,0:T(8,128)} custom-call(f32[16,8,128]{2,1,0:T(8,128)S(1)} %copy-done.4, f32[4,36,16,128]{3,2,1,0:T(8,128)S(1)} %get-tuple-element.28.upper_halo, bf16[128,4,128]{2,1,0:T(4,128)(2,1)S(1)} %all-to-all-done.pieces, f32[16,16,128]{2,1,0:T(8,128)S(1)} %get-tuple-element.30.far, bf16[128,512]{1,0:T(8,128)(2,1)S(1)} %copy-done.1, ...), custom_call_target="tpu_custom_call" | custom-call | flops 4000000000 | bytes 4194304 | tf_op jit(solution)/shard_map/final/pallas_call | solution.py:546
  (1 shorter events, 0.0 us)
Async XLA Ops:
  2.6 13.6 %collective-permute-start = (bf16[28,16,128]{2,1,0:T(8,128)(2,1)}, bf16[28,16,128]{2,1,0:T(8,128)(2,1)S(1)}, u32[]{:S(2)}, u32[]{:S(2)}) collective-permute-start(bf16[28,16,128]{2,1,0:T(8,128)(2,1)} %get-tuple-element.21), channel_id=1, source_target_pairs={{0,8},{8,16},{16,24},{24,32},{32,40},{40,48},{48,56},{56,64},{64,7... | collective-permute-start | bytes 344072 | tf_op jit(solution)/shard_map/ppermute | solution.py:488
  5.1 11.1 %collective-permute-start.1 = (bf16[28,16,128]{2,1,0:T(8,128)(2,1)}, bf16[28,16,128]{2,1,0:T(8,128)(2,1)S(1)}, u32[]{:S(2)}, u32[]{:S(2)}) collective-permute-start(bf16[28,16,128]{2,1,0:T(8,128)(2,1)} %get-tuple-element.22), channel_id=1, source_target_pairs={{8,0},{16,8},{24,16},{32,24},{40,32},{48,40},{56,48},{64,56},{72,6... | collective-permute-start | bytes 344072 | tf_op jit(solution)/shard_map/ppermute | solution.py:489
  9.5 6.7 %copy-start.3 = (bf16[48,16,128]{2,1,0:T(8,128)(2,1)S(1)}, bf16[48,16,128]{2,1,0:T(8,128)(2,1)}, u32[]{:S(2)}) copy-start(bf16[48,16,128]{2,1,0:T(8,128)(2,1)} %get-tuple-element.20.own) | copy-start | bytes 589828
  9.5 16.6 %all-to-all-start = ((bf16[128,4,128]{2,1,0:T(4,128)(2,1)}), bf16[128,4,128]{2,1,0:T(4,128)(2,1)S(1)}, u32[]{:S(2)}, u32[]{:S(2)}) async-start(bf16[128,4,128]{2,1,0:T(4,128)(2,1)} %pass.1), calls=%async_computation | async-start | bytes 262144 | tf_op jit(solution)/shard_map/all_to_all | solution.py:500
  16.2 1.7 %copy-start.2 = (f32[2,7,7,128]{3,0,2,1:T(2,128)S(1)}, f32[2,7,7,128]{3,0,2,1:T(2,128)}, u32[]{:S(2)}) copy-start(f32[2,7,7,128]{3,0,2,1:T(2,128)} %param.13) | copy-start | bytes 150532
  16.3 6.2 %collective-permute-start.2 = (bf16[70,16,128]{2,1,0:T(8,128)(2,1)S(1)}, bf16[70,16,128]{2,1,0:T(8,128)(2,1)S(1)}, u32[]{:S(2)}, u32[]{:S(2)}) collective-permute-start(bf16[70,16,128]{2,1,0:T(8,128)(2,1)S(1)} %get-tuple-element.23), channel_id=1, source_target_pairs={{0,1},{1,2},{2,3},{3,4},{4,5},{5,6},{6,7},{7,0},{8,9},{9,10},{10,1... | collective-permute-start | bytes 860168 | tf_op jit(solution)/shard_map/ppermute | solution.py:510
  17.9 6.7 %collective-permute-start.3 = (bf16[70,16,128]{2,1,0:T(8,128)(2,1)S(1)}, bf16[70,16,128]{2,1,0:T(8,128)(2,1)S(1)}, u32[]{:S(2)}, u32[]{:S(2)}) collective-permute-start(bf16[70,16,128]{2,1,0:T(8,128)(2,1)S(1)} %get-tuple-element.24), channel_id=1, source_target_pairs={{1,0},{2,1},{3,2},{4,3},{5,4},{6,5},{7,6},{0,7},{9,8},{10,9},{11,1... | collective-permute-start | bytes 860168 | tf_op jit(solution)/shard_map/ppermute | solution.py:511
  24.6 1.5 %copy-start = (bf16[2,4,4,128,128]{4,3,2,1,0:T(8,128)(2,1)S(1)}, bf16[2,4,4,128,128]{4,3,2,1,0:T(8,128)(2,1)}, u32[]{:S(2)}) copy-start(bf16[2,4,4,128,128]{4,3,2,1,0:T(8,128)(2,1)} %rad.1) | copy-start | bytes 3145732
  24.6 1.5 %copy-start.1 = (bf16[128,512]{1,0:T(8,128)(2,1)S(1)}, bf16[128,512]{1,0:T(8,128)(2,1)}, u32[]{:S(2)}) copy-start(bf16[128,512]{1,0:T(8,128)(2,1)} %anterp.1) | copy-start | bytes 393220
  24.6 1.5 %copy-start.4 = (f32[16,8,128]{2,1,0:T(8,128)S(1)}, f32[16,8,128]{2,1,0:T(8,128)}, u32[]{:S(2)}) copy-start(f32[16,8,128]{2,1,0:T(8,128)} %get-tuple-element.19.live) | copy-start | bytes 196612
  24.6 1.5 %copy-start.5 = (f32[8,512]{1,0:T(8,128)S(1)}, f32[8,512]{1,0:T(8,128)}, u32[]{:S(2)}) copy-start(f32[8,512]{1,0:T(8,128)} %get-tuple-element.31.phase) | copy-start | bytes 49156

commit v4 on v3

--- a/solution.py
+++ b/solution.py
@@ -248,7 +248,7 @@
             first = 2 - 2 * big_j
             total = translate(
                 lambda r, c: leaf_halo[(big_i * 2 + r) * 4 + c - first],
-                lambda part, dx, dy: trans_leaf[dx + 3, dy + 3, pl.ds(part, 1), :],
+                lambda dx, dy: leaf_coef(trans_leaf, dx, dy),
                 {},
                 range(first, first + 4),
             )
@@ -272,29 +272,38 @@
 
 
 def translate(source, coef, start, cols):
-    total = dict(start)
-    for dx in range(-3, 4):
-        for dy in range(-3, 4):
-            if max(abs(dx), abs(dy)) < 2:
-                continue
-            k_re = k_im = None
-            for a in range(2):
-                for b in range(2):
-                    r, c = dx + 2 + a, dy + 2 + b
-                    if not 0 <= r < 6 or c not in cols:
-                        continue
-                    if k_re is None:
-                        k_re = jnp.broadcast_to(coef(0, dx, dy), (8, 128))
-                        k_im = jnp.broadcast_to(coef(1, dx, dy), (8, 128))
-                    unit = source(r, c)
-                    s_re, s_im = unit[0:8], unit[8:16]
-                    t_re = k_re * s_re - k_im * s_im
-                    t_im = k_re * s_im + k_im * s_re
-                    if (a, b) in total:
-                        old_re, old_im = total[a, b]
-                        t_re, t_im = old_re + t_re, old_im + t_im
-                    total[a, b] = (t_re, t_im)
+    sums = {}
+    for r in range(6):
+        units = {}
+        for c in cols:
+            unit = source(r, c)
+            s_re, s_im = unit[0:8], unit[8:16]
+            units[c] = (s_re + s_im, s_im, s_re)
+        for a in range(2):
+            dx = r - 2 - a
+            for dy in range(-3, 4):
+                targets = [b for b in range(2) if dy + 2 + b in units]
+                if max(abs(dx), abs(dy)) < 2 or not targets:
+                    continue
+                factors = [jnp.broadcast_to(k, (8, 128)) for k in coef(dx, dy)]
+                for b in targets:
+                    terms = [k * v for k, v in zip(factors, units[dy + 2 + b])]
+                    if (a, b) in sums:
+                        terms = [old + new for old, new in zip(sums[a, b], terms)]
+                    sums[a, b] = terms
+    total = {}
+    for key, (p, q, w) in sums.items():
+        t_re, t_im = p - q, p + w
+        if key in start:
+            t_re, t_im = start[key][0] + t_re, start[key][1] + t_im
+        total[key] = (t_re, t_im)
     return total
+
+
+def leaf_coef(trans_leaf, dx, dy):
+    k_re = trans_leaf[dx + 3, dy + 3, pl.ds(0, 1), :]
+    k_im = trans_leaf[dx + 3, dy + 3, pl.ds(1, 1), :]
+    return k_re, k_re + k_im, k_im - k_re
 
 
 CHILDREN = [(a, b) for a in range(2) for b in range(2)]
@@ -351,7 +360,7 @@
                 start[a, b] = (unit[0:8], unit[8:16])
             total = translate(
                 lambda r, c: leaf_halo[big_j, (big_i * 2 + r) * 2 + c - first],
-                lambda part, dx, dy: trans_leaf[dx + 3, dy + 3, pl.ds(part, 1), :],
+                lambda dx, dy: leaf_coef(trans_leaf, dx, dy),
                 start,
                 range(first, first + 2),
             )
@@ -392,37 +401,34 @@
     out_hbm,
     out,
     table,
-    top,
     out_sems,
 ):
     for t in range(4):
-        table[t] = pieces[pl.ds(t * 32, 32)].astype(F32).reshape(128, 128).T
-
-    def top_step(t, carry):
+        turned = pieces[pl.ds(t * 32, 32)].astype(F32).reshape(128, 128).T
+        k_re, k_im = turned[0:56], turned[56:112]
+        table[t, 0:56] = k_re
+        table[t, 56:112] = k_re + k_im
+        table[t, 112:168] = k_im - k_re
+
+    back = None
+    for t in range(4):
         total = translate(
             lambda r, c: upper_halo[t, r * 6 + c],
-            lambda part, dx, dy: table[t, pl.ds((part * 7 + dx + 3) * 8 + dy + 3, 1), :],
+            lambda dx, dy: [
+                table[t, pl.ds(part * 56 + (dx + 3) * 8 + dy + 3, 1), :] for part in range(3)
+            ],
             {},
             range(6),
         )
-        for a, b in CHILDREN:
-            top[t, a * 2 + b] = pair(*total[a, b]).astype(BF16).astype(F32)
-        return carry
-
-    lax.fori_loop(0, 4, top_step, 0)
-
-    rows = []
-    for quad in range(4):
-        for child in range(4):
-            tiles = []
-            for t in range(4):
-                unit = top[t, quad]
-                t_re, t_im = unit[0:8], unit[8:16]
+        rows = []
+        for key in CHILDREN:
+            t_re, t_im = (part.astype(BF16).astype(F32) for part in total[key])
+            for child in range(4):
                 c = phase[child : child + 1, t * 128 : (t + 1) * 128]
                 s = phase[4 + child : 5 + child, t * 128 : (t + 1) * 128]
-                tiles.append(pair(c * t_re + s * t_im, c * t_im - s * t_re).astype(BF16))
-            rows.append(jnp.concatenate(tiles, axis=1))
-    back = dot_nt(jnp.concatenate(rows, axis=0), anterp[...])
+                rows.append(pair(c * t_re + s * t_im, c * t_im - s * t_re).astype(BF16))
+        part = dot_nt(jnp.concatenate(rows, axis=0), anterp[:, t * 128 : (t + 1) * 128])
+        back = part if back is None else back + part
     sent = []
     for i in range(4):
         for j in range(4):
@@ -540,7 +546,7 @@
         out_specs=(vmem(),) * 3,
         scratch_shapes=[pltpu.VMEM((2, 16, 16, 128), F32)],
         compiler_params=params(48),
-        cost_estimate=cost(2),
+        cost_estimate=pl.CostEstimate(flops=10**7, bytes_accessed=1 << 14, transcendentals=0),
         name="middle",
     )(own, before, after, left, right, by_offset, near, rest, far)
     return pl.pallas_call(
@@ -550,8 +556,7 @@
         out_specs=hbm(),
         scratch_shapes=[
             pltpu.VMEM((2, 4, 4, 8, 128), F32),
-            pltpu.VMEM((4, 128, 128), F32),
-            pltpu.VMEM((4, 4, 16, 128), F32),
+            pltpu.VMEM((4, 168, 128), F32),
             pltpu.SemaphoreType.DMA((4,)),
         ],
         compiler_params=params(48),

time: 28.1 us -> 28 us (level)
  no operation moved by 1% of the time
where the time goes in v4:
time: 28 us; the launch traced here: 27.9 us
  starting transfers between devices  15.2 us (54%)
  Pallas kernels  9.82 us (35%)
  waiting for transfers between devices  2.65 us (9%)
    all_to_all x1, starting transfers between devices, shards(): lax.all_to_all(pieces, ('box', 'dir'), split_axis=0, concat_axis=0, tiled...  6.66 us
    pallas_call x1, Pallas kernels, shards(): pl.pallas_call(near_kernel, out_shape=(jax.ShapeDtypeStruct((16, 16, 128)...  4.53 us
    ppermute x1, starting transfers between devices, shards(): after = lax.ppermute(to_before, 'box', backward)  4.4 us
    pallas_call x1, Pallas kernels, shards(): pl.pallas_call(leaf_kernel, out_shape=outputs, in_specs=[hbm()] * 6, out_...  2.56 us
    ppermute x1, starting transfers between devices, shards(): before = lax.ppermute(to_after, 'box', forward)  2.53 us
    ppermute x1, waiting for transfers between devices, shards(): lax.ppermute(to_left, 'dir', [((i + 1) % n_dir, i) for i in range(n_dir)])  2.07 us
    pallas_call x1, Pallas kernels, shards(): pl.pallas_call(final_kernel, out_shape=jax.ShapeDtypeStruct((2, 4, 4, 8,...  1.72 us
    ppermute x1, starting transfers between devices, shards(): lax.ppermute(to_right, 'dir', [(i, (i + 1) % n_dir) for i in range(n_dir)])  1.65 us
  transfers between devices with their start and end apart: 5, of which 2 were waited for; matrix products, arithmetic and copies ran while one was open for 0% of the time, Pallas kernels for 20%

profile of v4, /device:TPU:1, one launch (start us, length us, event | category | flops | bytes accessed | tf_op | source)
XLA Modules:
  0.0 27.9 jit_solution(1181963558535570749)
XLA Ops:
  0.0 2.6 %leaf.1 = (bf16[48,16,128]{2,1,0:T(8,128)(2,1)}, bf16[28,16,128]{2,1,0:T(8,128)(2,1)}, bf16[28,16,128]{2,1,0:T(8,128)(2,1)}, f32[8,512]{1,0:T(8,128)}, f32[16,8,...) custom-call(s32[4,4]{1,0:T(4,128)} %counts_hbm.1, bf16[2,4,4,8,128]{4,3,2,1,0:T(8,128)(2,1)} %coeffs_hbm.1, ...), custom_call_target="tpu_custom_call" | custom-call | flops 2000000000 | bytes 2097152 | tf_op jit(solution)/shard_map/leaf/pallas_call | solution.py:469
  2.6 2.5 %collective-permute-start = (bf16[28,16,128]{2,1,0:T(8,128)(2,1)}, bf16[28,16,128]{2,1,0:T(8,128)(2,1)S(1)}, u32[]{:S(2)}, u32[]{:S(2)}) collective-permute-start(bf16[28,16,128]{2,1,0:T(8,128)(2,1)} %get-tuple-element.21), channel_id=1, source_target_pairs={{0,8},{8,16},{16,24},{24,32},{32,40},{40,48},{48,56},{56,64},{64,7... | collective-permute-start | bytes 344072 | tf_op jit(solution)/shard_map/ppermute | solution.py:494
  5.1 4.4 %collective-permute-start.1 = (bf16[28,16,128]{2,1,0:T(8,128)(2,1)}, bf16[28,16,128]{2,1,0:T(8,128)(2,1)S(1)}, u32[]{:S(2)}, u32[]{:S(2)}) collective-permute-start(bf16[28,16,128]{2,1,0:T(8,128)(2,1)} %get-tuple-element.22), channel_id=1, source_target_pairs={{8,0},{16,8},{24,16},{32,24},{40,32},{48,40},{56,48},{64,56},{72,6... | collective-permute-start | bytes 344072 | tf_op jit(solution)/shard_map/ppermute | solution.py:495
  9.5 0.0 copy-start
  9.5 6.7 %all-to-all-start = ((bf16[128,4,128]{2,1,0:T(4,128)(2,1)}), bf16[128,4,128]{2,1,0:T(4,128)(2,1)S(1)}, u32[]{:S(2)}, u32[]{:S(2)}) async-start(bf16[128,4,128]{2,1,0:T(4,128)(2,1)} %pass.1), calls=%async_computation | async-start | bytes 262144 | tf_op jit(solution)/shard_map/all_to_all | solution.py:506
  16.2 0.0 collective-permute-done.before
  16.2 0.0 collective-permute-done.1.after
  16.2 0.0 copy-done
  16.2 0.0 copy-start.1
  16.2 0.1 pack.1
  16.3 1.6 %collective-permute-start.2 = (bf16[70,16,128]{2,1,0:T(8,128)(2,1)S(1)}, bf16[70,16,128]{2,1,0:T(8,128)(2,1)S(1)}, u32[]{:S(2)}, u32[]{:S(2)}) collective-permute-start(bf16[70,16,128]{2,1,0:T(8,128)(2,1)S(1)} %get-tuple-element.23), channel_id=1, source_target_pairs={{0,1},{1,2},{2,3},{3,4},{4,5},{5,6},{6,7},{7,0},{8,9},{9,10},{10,1... | collective-permute-start | bytes 860168 | tf_op jit(solution)/shard_map/ppermute | solution.py:516
  17.9 0.0 collective-permute-start.3
  17.9 0.0 copy-done.1
  17.9 4.5 %near.1 = (f32[16,16,128]{2,1,0:T(8,128)S(1)}, bf16[6,2,4,128,128]{4,3,2,1,0:T(8,128)(2,1)S(1)}, f32[16,16,128]{2,1,0:T(8,128)S(1)}) custom-call(bf16[48,16,128]{2,1,0:T(8,128)(2,1)S(1)} %copy-done, bf16[28,16,128]{2,1,0:T(8,128)(2,1)S(1)} %collective-permute-done.before, bf16[28,16,128]{2,1,0:T(8,128)(2,1)S(1)} %collective-permute-done.1.after, ...), custom_call_target="tpu_custom_call" | custom-call | flops 4000000000 | bytes 4194304 | tf_op jit(solution)/shard_map/near/pallas_call | solution.py:519
  22.5 0.0 copy-start.2
  22.5 0.0 copy-start.3
  22.5 0.0 copy-start.4
  22.5 0.0 copy-start.5
  22.5 0.0 collective-permute-done.2.left
  22.5 2.1 %collective-permute-done.3.right = bf16[70,16,128]{2,1,0:T(8,128)(2,1)S(1)} collective-permute-done((bf16[70,16,128]{2,1,0:T(8,128)(2,1)S(1)}, bf16[70,16,128]{2,1,0:T(8,128)(2,1)S(1)}, u32[]{:S(2)}, u32[]{:S(2)}) %collective-permute-start.3) | collective-permute-done | bytes 286752 | tf_op jit(solution)/shard_map/ppermute | solution.py:517
  24.6 0.9 %middle.1 = (f32[16,16,128]{2,1,0:T(8,128)S(1)}, f32[4,36,16,128]{3,2,1,0:T(8,128)S(1)}, f32[16,16,128]{2,1,0:T(8,128)S(1)}) custom-call(bf16[48,16,128]{2,1,0:T(8,128)(2,1)S(1)} %copy-done, bf16[28,16,128]{2,1,0:T(8,128)(2,1)S(1)} %collective-permute-done.before, bf16[28,16,128]{2,1,0:T(8,128)(2,1)S(1)} %collective-permute-done.1.after, ...), custom_call_target="tpu_custom_call" | custom-call | flops 10000000 | bytes 16384 | tf_op jit(solution)/shard_map/middle/pallas_call | solution.py:538
  25.5 0.6 %all-to-all-done.pieces = bf16[128,4,128]{2,1,0:T(4,128)(2,1)S(1)} async-done(((bf16[128,4,128]{2,1,0:T(4,128)(2,1)}), bf16[128,4,128]{2,1,0:T(4,128)(2,1)S(1)}, u32[]{:S(2)}, u32[]{:S(2)}) %all-to-all-start) | async-done | bytes 131104 | tf_op jit(solution)/shard_map/all_to_all | solution.py:506
  26.1 0.0 copy-done.2
  26.1 0.0 copy-done.3
  26.1 0.0 copy-done.4
  26.1 0.0 copy-done.5
  26.1 1.7 %final.1 = f32[2,4,4,8,128]{4,3,2,1,0:T(8,128)} custom-call(f32[16,8,128]{2,1,0:T(8,128)S(1)} %copy-done.4, f32[4,36,16,128]{3,2,1,0:T(8,128)S(1)} %get-tuple-element.28.upper_halo, bf16[128,4,128]{2,1,0:T(4,128)(2,1)S(1)} %all-to-all-done.pieces, f32[16,16,128]{2,1,0:T(8,128)S(1)} %get-tuple-element.30.far, bf16[128,512]{1,0:T(8,128)(2,1)S(1)} %copy-done.3, ...), custom_call_target="tpu_custom_call" | custom-call | flops 4000000000 | bytes 4194304 | tf_op jit(solution)/shard_map/final/pallas_call | solution.py:552
  (1 shorter events, 0.0 us)
Async XLA Ops:
  2.6 13.6 %collective-permute-start = (bf16[28,16,128]{2,1,0:T(8,128)(2,1)}, bf16[28,16,128]{2,1,0:T(8,128)(2,1)S(1)}, u32[]{:S(2)}, u32[]{:S(2)}) collective-permute-start(bf16[28,16,128]{2,1,0:T(8,128)(2,1)} %get-tuple-element.21), channel_id=1, source_target_pairs={{0,8},{8,16},{16,24},{24,32},{32,40},{40,48},{48,56},{56,64},{64,7... | collective-permute-start | bytes 344072 | tf_op jit(solution)/shard_map/ppermute | solution.py:494
  5.1 11.1 %collective-permute-start.1 = (bf16[28,16,128]{2,1,0:T(8,128)(2,1)}, bf16[28,16,128]{2,1,0:T(8,128)(2,1)S(1)}, u32[]{:S(2)}, u32[]{:S(2)}) collective-permute-start(bf16[28,16,128]{2,1,0:T(8,128)(2,1)} %get-tuple-element.22), channel_id=1, source_target_pairs={{8,0},{16,8},{24,16},{32,24},{40,32},{48,40},{56,48},{64,56},{72,6... | collective-permute-start | bytes 344072 | tf_op jit(solution)/shard_map/ppermute | solution.py:495
  9.5 6.7 %copy-start = (bf16[48,16,128]{2,1,0:T(8,128)(2,1)S(1)}, bf16[48,16,128]{2,1,0:T(8,128)(2,1)}, u32[]{:S(2)}) copy-start(bf16[48,16,128]{2,1,0:T(8,128)(2,1)} %get-tuple-element.20.own) | copy-start | bytes 589828
  9.5 16.6 %all-to-all-start = ((bf16[128,4,128]{2,1,0:T(4,128)(2,1)}), bf16[128,4,128]{2,1,0:T(4,128)(2,1)S(1)}, u32[]{:S(2)}, u32[]{:S(2)}) async-start(bf16[128,4,128]{2,1,0:T(4,128)(2,1)} %pass.1), calls=%async_computation | async-start | bytes 262144 | tf_op jit(solution)/shard_map/all_to_all | solution.py:506
  16.2 1.7 %copy-start.1 = (f32[2,7,7,128]{3,0,2,1:T(2,128)S(1)}, f32[2,7,7,128]{3,0,2,1:T(2,128)}, u32[]{:S(2)}) copy-start(f32[2,7,7,128]{3,0,2,1:T(2,128)} %param.13) | copy-start | bytes 150532
  16.3 6.2 %collective-permute-start.2 = (bf16[70,16,128]{2,1,0:T(8,128)(2,1)S(1)}, bf16[70,16,128]{2,1,0:T(8,128)(2,1)S(1)}, u32[]{:S(2)}, u32[]{:S(2)}) collective-permute-start(bf16[70,16,128]{2,1,0:T(8,128)(2,1)S(1)} %get-tuple-element.23), channel_id=1, source_target_pairs={{0,1},{1,2},{2,3},{3,4},{4,5},{5,6},{6,7},{7,0},{8,9},{9,10},{10,1... | collective-permute-start | bytes 860168 | tf_op jit(solution)/shard_map/ppermute | solution.py:516
  17.9 6.7 %collective-permute-start.3 = (bf16[70,16,128]{2,1,0:T(8,128)(2,1)S(1)}, bf16[70,16,128]{2,1,0:T(8,128)(2,1)S(1)}, u32[]{:S(2)}, u32[]{:S(2)}) collective-permute-start(bf16[70,16,128]{2,1,0:T(8,128)(2,1)S(1)} %get-tuple-element.24), channel_id=1, source_target_pairs={{1,0},{2,1},{3,2},{4,3},{5,4},{6,5},{7,6},{0,7},{9,8},{10,9},{11,1... | collective-permute-start | bytes 860168 | tf_op jit(solution)/shard_map/ppermute | solution.py:517
  22.5 3.6 %copy-start.2 = (bf16[2,4,4,128,128]{4,3,2,1,0:T(8,128)(2,1)S(1)}, bf16[2,4,4,128,128]{4,3,2,1,0:T(8,128)(2,1)}, u32[]{:S(2)}) copy-start(bf16[2,4,4,128,128]{4,3,2,1,0:T(8,128)(2,1)} %rad.1) | copy-start | bytes 3145732
  22.5 3.6 %copy-start.3 = (bf16[128,512]{1,0:T(8,128)(2,1)S(1)}, bf16[128,512]{1,0:T(8,128)(2,1)}, u32[]{:S(2)}) copy-start(bf16[128,512]{1,0:T(8,128)(2,1)} %anterp.1) | copy-start | bytes 393220
  22.5 3.6 %copy-start.4 = (f32[16,8,128]{2,1,0:T(8,128)S(1)}, f32[16,8,128]{2,1,0:T(8,128)}, u32[]{:S(2)}) copy-start(f32[16,8,128]{2,1,0:T(8,128)} %get-tuple-element.19.live) | copy-start | bytes 196612
  22.5 3.6 %copy-start.5 = (f32[8,512]{1,0:T(8,128)S(1)}, f32[8,512]{1,0:T(8,128)}, u32[]{:S(2)}) copy-start(f32[8,512]{1,0:T(8,128)} %get-tuple-element.31.phase) | copy-start | bytes 49156
